TPU v7x, 32 devices: a whole 2x2x4 slice. The times are simulated.
32 devices in a mesh: seq: 16 (over z, x, core), head: 2 (over y).
Axes of the slice: x: 2, y: 2, z: 4, core: 2. Of those that a mesh axis runs over, the one named last changes fastest.
Arguments:
- rows: bfloat16 [16384, 768], P('seq'), may hold values from -6 to 6
- lengths: int32 [1], replicated, may hold values from 8192 to 16384, as said below
- norm_gains: float32 [2, 768], replicated, may hold values from 0.5 to 1.5
- norm_shifts: float32 [2, 768], replicated, may hold values from -2 to 2
- qkv_weight: bfloat16 [3, 768, 768], P(None, None, 'head'), may hold values from -0.21875 to 0.21875
- qv_bias: float32 [2, 768], P(None, 'head'), may hold values from -3 to 3
- out_weight: bfloat16 [768, 768], P('head'), may hold values from -2.5 to 2.5
- out_bias: float32 [768], replicated, may hold values from -2 to 2
- up_weight: bfloat16 [768, 3072], P(None, 'head'), may hold values from -0.21875 to 0.21875
- up_bias: float32 [3072], P('head'), may hold values from -3 to 3
- down_weight: bfloat16 [3072, 768], P('head'), may hold values from -0.109375 to 0.109375
- down_bias: float32 [768], replicated, may hold values from -2 to 2
- out_cot: bfloat16 [16384, 768], P('seq'), may hold values from -6 to 6
Outputs:
- out_rows: bfloat16 [16384, 768], P('seq')
- rows_grad: float32 [16384, 768], P('seq')
- norm_gains_grad: float32 [2, 768], replicated
- norm_shifts_grad: float32 [2, 768], replicated
- qkv_grad: float32 [3, 768, 768], P(None, None, 'head')
- qv_bias_grad: float32 [2, 768], P(None, 'head')
- out_weight_grad: float32 [768, 768], P('head')
- out_bias_grad: float32 [768], replicated
- up_weight_grad: float32 [768, 3072], P(None, 'head')
- up_bias_grad: float32 [3072], P('head')
- down_weight_grad: float32 [3072, 768], P('head')
- down_bias_grad: float32 [768], replicated
Inputs may be any that keep to these rules, and one draw needn't show every extreme that they name: Slide k uses the first lengths[k] rows of its block of 16384 rows; at least one slide uses all of its block.
All inputs are finite; a program needn't handle non-finite values.
Results may differ from a plain program's by a relative error of at most 0.015.
Values may be sent and summed in bfloat16 or wider, within the bound.
No kernel may reach another device: no remote copies, remote signals or barrier semaphores. Data moves between devices by JAX's collectives and lax.ppermute only.
A program may use at most 256 MiB of HBM per device.

v0:
```python
import math

import jax
import jax.numpy as jnp
from jax import lax
from jax.sharding import PartitionSpec as P

HD = 48
SEG = 1024


eps = 1e-05
neg_big = -1e30
levels = 5
root_half = 1.0 / math.sqrt(2.0)
density_norm = 1.0 / math.sqrt(2.0 * math.pi)


def for_sending(x):

    def short(part):
        return part.astype(jnp.bfloat16) if part.dtype == jnp.float32 else part

    return jax.tree.map(short, x)


def from_partner(block, axis, apart):
    count = lax.axis_size(axis)
    route = []
    for low in range(count):
        high = low | 1 << apart
        if high != low and high < count:
            route += [(low, high), (high, low)]
    return lax.ppermute(block, axis, route)


def norm_rows(value_rows, gain, shift):
    row_mean = jnp.mean(value_rows, -1, keepdims=True)
    centred = value_rows - row_mean
    inverse = lax.rsqrt(jnp.mean(centred * centred, -1, keepdims=True) + eps)
    unit_rows = centred * inverse
    return (unit_rows * gain + shift, unit_rows, inverse)


def norm_back(output_gradient, unit_rows, inverse, gain):
    scaled = output_gradient * gain
    inner_term = (
        scaled
        - jnp.mean(scaled, -1, keepdims=True)
        - unit_rows * jnp.mean(scaled * unit_rows, -1, keepdims=True)
    )
    return inverse * inner_term


def gelu_value(pre_act):
    return 0.5 * pre_act * (1.0 + jax.scipy.special.erf(pre_act * root_half))


def gelu_slope(pre_act):
    return (
        0.5 * (1.0 + jax.scipy.special.erf(pre_act * root_half))
        + pre_act * jnp.exp(-0.5 * pre_act * pre_act) * density_norm
    )


def select_rows(value_rows, picker, spacing):
    row_count, local_heads = (value_rows.shape[0], value_rows.shape[1])
    folded = value_rows.reshape((row_count // spacing, spacing) + value_rows.shape[1:])
    select_mask = picker.astype(value_rows.dtype).reshape(
        (1, spacing, local_heads) + (1,) * (value_rows.ndim - 2)
    )
    chosen = jnp.sum(folded * select_mask, axis=1)
    return jnp.moveaxis(chosen, 1, 0)


def place_rows(chosen, picker, spacing):
    moved_rows = jnp.moveaxis(chosen, 0, 1)
    select_mask = picker.reshape((1, spacing, picker.shape[1]) + (1,) * (moved_rows.ndim - 2))
    spread = moved_rows[:, None] * select_mask
    return spread.reshape((moved_rows.shape[0] * spacing,) + moved_rows.shape[1:])


def place_lse(chosen, picker):
    moved_rows = jnp.moveaxis(chosen, 0, 1)[:, None, :]
    spread = jnp.where(picker[None] > 0.5, moved_rows, neg_big)
    return spread.reshape(-1, picker.shape[1])


def masked_scores(query_rows, key_matrix, query_ok, key_ok):
    score_scale = 1.0 / math.sqrt(query_rows.shape[-1])
    raw_scores = (
        jnp.einsum("egy,ehy->egh", query_rows, key_matrix, preferred_element_type=jnp.float32)
        * score_scale
    )
    allowed = jnp.maximum(key_ok[:, None, :], 1.0 - query_ok[:, :, None]) > 0.5
    return jnp.where(allowed, raw_scores, neg_big)


def attend(pieces):
    query_rows, key_matrix, value_rows, query_ok, key_ok = pieces
    scores = masked_scores(query_rows, key_matrix, query_ok, key_ok)
    row_top = jnp.max(scores, -1, keepdims=True)
    weight_matrix = jnp.exp(scores - row_top)
    row_total = jnp.sum(weight_matrix, -1, keepdims=True)
    summed = jnp.einsum(
        "efw,ews->efs",
        weight_matrix.astype(jnp.bfloat16),
        value_rows,
        preferred_element_type=jnp.float32,
    )
    return (summed / row_total, (row_top + jnp.log(row_total))[..., 0])


def attend_back(pieces):
    query_rows, key_matrix, value_rows, query_ok, key_ok, output_gradient, whole_lse, inner_term = (
        pieces
    )
    score_scale = 1.0 / math.sqrt(query_rows.shape[-1])
    probability_rows = jnp.exp(
        masked_scores(query_rows, key_matrix, query_ok, key_ok) - whole_lse[..., None]
    )
    grad_values = jnp.einsum(
        "cwa,cwh->cah",
        probability_rows.astype(jnp.bfloat16),
        output_gradient,
        preferred_element_type=jnp.float32,
    )
    probability_gradient = jnp.einsum(
        "egy,ehy->egh", output_gradient, value_rows, preferred_element_type=jnp.float32
    )
    score_gradient = (probability_rows * (probability_gradient - inner_term[..., None])).astype(
        jnp.bfloat16
    )
    grad_queries = (
        jnp.einsum("efw,ews->efs", score_gradient, key_matrix, preferred_element_type=jnp.float32)
        * score_scale
    )
    grad_keys = (
        jnp.einsum("cwa,cwh->cah", score_gradient, query_rows, preferred_element_type=jnp.float32)
        * score_scale
    )
    return (grad_queries, grad_keys, grad_values)


def in_blocks(function, pieces, block_group):
    lead_rows = pieces[0].shape[0]
    shaped = tuple(
        (
            item_piece.reshape((lead_rows // block_group, block_group) + item_piece.shape[1:])
            for item_piece in pieces
        )
    )
    results = lax.map(function, shaped)
    return tuple((result.reshape((lead_rows,) + result.shape[2:]) for result in results))


def join_halves(own_piece, peer_piece, is_upper):
    return jnp.where(
        is_upper,
        jnp.concatenate([peer_piece, own_piece], 1),
        jnp.concatenate([own_piece, peer_piece], 1),
    )


def gather_keys(item_sets, groups):
    seq_place = lax.axis_index("seq")
    item_sets = list(item_sets)
    for bit_index in range(max(groups).bit_length() - 1):
        active = [
            slot_index for slot_index in range(len(item_sets)) if groups[slot_index] > 2**bit_index
        ]
        send_list = tuple(
            (item_piece for slot_index in active for item_piece in item_sets[slot_index])
        )
        received = jax.tree.map(
            lambda part, own: part.astype(own.dtype),
            from_partner(for_sending(send_list), "seq", bit_index),
            send_list,
        )
        is_upper = seq_place // 2**bit_index % 2 == 1
        for position, slot_index in enumerate(active):
            peer_set = received[3 * position : 3 * position + 3]
            item_sets[slot_index] = tuple(
                (
                    join_halves(own_piece, peer_piece, is_upper)
                    for own_piece, peer_piece in zip(item_sets[slot_index], peer_set)
                )
            )
    return item_sets


def gather_again(item_sets, groups):
    seq_place = lax.axis_index("seq")
    item_sets = list(item_sets)
    for bit_index in range(max(groups).bit_length() - 1):
        active = [
            slot_index for slot_index in range(len(item_sets)) if groups[slot_index] > 2**bit_index
        ]
        send_list = tuple(
            (item_piece for slot_index in active for item_piece in item_sets[slot_index])
        )
        received = jax.tree.map(
            lambda part, own: part.astype(own.dtype),
            from_partner(for_sending(send_list), "seq", bit_index),
            send_list,
        )
        is_upper = seq_place // 2**bit_index % 2 == 1
        for position, slot_index in enumerate(active):
            peer_set = received[3 * position : 3 * position + 3]
            item_sets[slot_index] = tuple(
                (
                    join_halves(own_piece, peer_piece, is_upper)
                    for own_piece, peer_piece in zip(item_sets[slot_index], peer_set)
                )
            )
    return item_sets


def scatter_key_grads(item_sets, groups):
    seq_place = lax.axis_index("seq")
    item_sets = list(item_sets)
    for bit_index in reversed(range(max(groups).bit_length() - 1)):
        active = [
            slot_index for slot_index in range(len(item_sets)) if groups[slot_index] > 2**bit_index
        ]
        is_upper = seq_place // 2**bit_index % 2 == 1
        keep_list = []
        send_list = []
        for slot_index in active:
            for item_piece in item_sets[slot_index]:
                half_rows = item_piece.shape[1] // 2
                lower_part = item_piece[:, :half_rows]
                upper_part = item_piece[:, half_rows:]
                keep_list.append(jnp.where(is_upper, upper_part, lower_part))
                send_list.append(jnp.where(is_upper, lower_part, upper_part))
        received = from_partner(for_sending(tuple(send_list)), "seq", bit_index)
        for position, slot_index in enumerate(active):
            item_sets[slot_index] = (
                keep_list[2 * position] + received[2 * position],
                keep_list[2 * position + 1] + received[2 * position + 1],
            )
    return item_sets


def local(
    rows,
    lengths,
    norm_gains,
    norm_shifts,
    qkv_weight,
    qv_bias,
    out_weight,
    out_bias,
    up_weight,
    up_bias,
    down_weight,
    down_bias,
    out_cot,
):
    row_count = rows.shape[0]
    local_width = qkv_weight.shape[2]
    local_heads = local_width // HD
    head_base = lax.axis_index("head") * local_heads
    slide_rows = min(16 * SEG, row_count * lax.axis_size("seq"))
    places = lax.axis_index("seq") * row_count + jnp.arange(row_count, dtype=jnp.int32)
    slide_of = places // slide_rows
    slide_len = jnp.sum(
        jnp.where(
            slide_of[:, None] == jnp.arange(lengths.shape[0], dtype=jnp.int32)[None, :],
            lengths[None, :],
            0,
        ),
        axis=1,
    )
    present = (places % slide_rows < slide_len).astype(jnp.float32)
    present_heads = jnp.broadcast_to(present[:, None], (row_count, local_heads))
    inputs = rows.astype(jnp.float32)
    normed1, unit1, inverse1 = norm_rows(inputs, norm_gains[0], norm_shifts[0])
    normed1_low = normed1.astype(jnp.bfloat16)
    projected = jnp.einsum(
        "td,cde->cte", normed1_low, qkv_weight, preferred_element_type=jnp.float32
    )
    query_rows = (
        (projected[0] + qv_bias[0]).astype(jnp.bfloat16).reshape(row_count, local_heads, HD)
    )
    key_matrix = projected[1].astype(jnp.bfloat16).reshape(row_count, local_heads, HD)
    value_rows = (
        (projected[2] + qv_bias[1]).astype(jnp.bfloat16).reshape(row_count, local_heads, HD)
    )
    branch_plans = []
    groups = []
    local_sets = []
    for level_index in range(levels):
        spacing = 2**level_index
        seg_span = min(SEG * spacing, slide_rows)
        picker = (
            jnp.arange(spacing)[:, None] == (head_base + jnp.arange(local_heads))[None, :] % spacing
        ).astype(jnp.float32)
        branch_plans.append((spacing, seg_span, picker))
        groups.append(max(seg_span // row_count, 1))
        local_sets.append(
            (
                select_rows(key_matrix, picker, spacing),
                select_rows(value_rows, picker, spacing),
                select_rows(present_heads, picker, spacing).astype(jnp.bfloat16),
            )
        )
    gathered = gather_keys(local_sets, groups)

    def branch_inputs(level_index, key_sets):
        spacing, seg_span, picker = branch_plans[level_index]
        segments = max(row_count // seg_span, 1)
        batch_size = local_heads * segments
        query_count = row_count // spacing // segments
        block_group = min(batch_size, max(1, 512 // query_count))
        key_set, value_set, key_ok = key_sets[level_index]
        pieces = (
            select_rows(query_rows, picker, spacing),
            key_set,
            value_set,
            select_rows(present_heads, picker, spacing),
            key_ok.astype(jnp.float32),
        )
        return (pieces, batch_size, query_count, block_group)

    out_parts = []
    lse_parts = []
    for level_index in range(levels):
        spacing, seg_span, picker = branch_plans[level_index]
        pieces, batch_size, query_count, block_group = branch_inputs(level_index, gathered)
        chosen_out, chosen_lse = in_blocks(attend, pieces, block_group)
        out_parts.append(place_rows(chosen_out, picker, spacing))
        lse_parts.append(place_lse(chosen_lse, picker))
    stacked = jnp.stack(lse_parts)
    row_top = jnp.max(stacked, 0)
    shares = jnp.exp(stacked - row_top)
    share_total = jnp.sum(shares, 0)
    merged = jnp.sum(shares[..., None] * jnp.stack(out_parts), 0) / share_total[..., None]
    whole_lse = row_top + jnp.log(share_total)
    merged_low = merged.reshape(row_count, local_width).astype(jnp.bfloat16)
    attended = (
        lax.psum(
            jnp.dot(merged_low, out_weight, preferred_element_type=jnp.float32).astype(
                jnp.bfloat16
            ),
            "head",
        ).astype(jnp.float32)
        + out_bias
    )
    hidden = inputs + attended
    normed2, unit2, inverse2 = norm_rows(hidden, norm_gains[1], norm_shifts[1])
    normed2_low = normed2.astype(jnp.bfloat16)
    pre_act = jnp.dot(normed2_low, up_weight, preferred_element_type=jnp.float32) + up_bias
    activated = gelu_value(pre_act).astype(jnp.bfloat16)
    mlp_out = (
        lax.psum(
            jnp.dot(activated, down_weight, preferred_element_type=jnp.float32).astype(
                jnp.bfloat16
            ),
            "head",
        ).astype(jnp.float32)
        + down_bias
    )
    out_rows = (hidden + mlp_out).astype(jnp.bfloat16)
    cot_rows = out_cot.astype(jnp.float32)
    down_weight_grad = jnp.einsum(
        "tf,td->fd", activated, out_cot, preferred_element_type=jnp.float32
    )
    down_bias_grad = jnp.sum(cot_rows, 0)
    grad_act = jnp.einsum("td,fd->tf", out_cot, down_weight, preferred_element_type=jnp.float32)
    grad_pre = grad_act * gelu_slope(pre_act)
    up_bias_grad = jnp.sum(grad_pre, 0)
    grad_pre_low = grad_pre.astype(jnp.bfloat16)
    up_weight_grad = jnp.einsum(
        "td,tf->df", normed2_low, grad_pre_low, preferred_element_type=jnp.float32
    )
    grad_normed2 = lax.psum(
        jnp.einsum("tf,df->td", grad_pre_low, up_weight, preferred_element_type=jnp.float32).astype(
            jnp.bfloat16
        ),
        "head",
    ).astype(jnp.float32)
    grad_hidden = cot_rows + norm_back(grad_normed2, unit2, inverse2, norm_gains[1])
    second_gain_grad = jnp.sum(grad_normed2 * unit2, 0)
    second_shift_grad = jnp.sum(grad_normed2, 0)
    out_bias_grad = jnp.sum(grad_hidden, 0)
    grad_attended_low = grad_hidden.astype(jnp.bfloat16)
    out_weight_grad = jnp.einsum(
        "te,td->ed", merged_low, grad_attended_low, preferred_element_type=jnp.float32
    )
    grad_merged = (
        jnp.einsum("td,ed->te", grad_attended_low, out_weight, preferred_element_type=jnp.float32)
        .astype(jnp.bfloat16)
        .reshape(row_count, local_heads, HD)
    )
    inner_rows = jnp.sum(grad_merged.astype(jnp.float32) * merged, -1)
    back_sets = gather_again(local_sets, groups)
    grad_query_rows = jnp.zeros((row_count, local_heads, HD), jnp.float32)
    key_grad_sets = []
    for level_index in range(levels):
        spacing, seg_span, picker = branch_plans[level_index]
        pieces, batch_size, query_count, block_group = branch_inputs(level_index, back_sets)
        extra = (
            select_rows(grad_merged, picker, spacing),
            select_rows(whole_lse, picker, spacing),
            select_rows(inner_rows, picker, spacing),
        )
        grad_queries, grad_keys, grad_values = in_blocks(attend_back, pieces + extra, block_group)
        grad_query_rows = grad_query_rows + place_rows(grad_queries, picker, spacing)
        key_grad_sets.append((grad_keys, grad_values))
    owned = scatter_key_grads(key_grad_sets, groups)
    grad_key_rows = jnp.zeros((row_count, local_heads, HD), jnp.float32)
    grad_value_rows = jnp.zeros((row_count, local_heads, HD), jnp.float32)
    for level_index in range(levels):
        spacing, seg_span, picker = branch_plans[level_index]
        grad_key_rows = grad_key_rows + place_rows(owned[level_index][0], picker, spacing)
        grad_value_rows = grad_value_rows + place_rows(owned[level_index][1], picker, spacing)
    grad_stack = jnp.stack([grad_query_rows, grad_key_rows, grad_value_rows]).reshape(
        3, row_count, local_width
    )
    qv_bias_grad = jnp.stack([jnp.sum(grad_stack[0], 0), jnp.sum(grad_stack[2], 0)])
    grad_stack_low = grad_stack.astype(jnp.bfloat16)
    qkv_grad = jnp.einsum(
        "td,cte->cde", normed1_low, grad_stack_low, preferred_element_type=jnp.float32
    )
    grad_normed1 = lax.psum(
        jnp.einsum(
            "cte,cde->td", grad_stack_low, qkv_weight, preferred_element_type=jnp.float32
        ).astype(jnp.bfloat16),
        "head",
    ).astype(jnp.float32)
    rows_grad = grad_hidden + norm_back(grad_normed1, unit1, inverse1, norm_gains[0])
    first_gain_grad = jnp.sum(grad_normed1 * unit1, 0)
    first_shift_grad = jnp.sum(grad_normed1, 0)
    (
        qkv_grad,
        qv_bias_grad,
        out_weight_grad,
        out_bias_grad,
        first_gain_grad,
        first_shift_grad,
        down_weight_grad,
        down_bias_grad,
        up_weight_grad,
        up_bias_grad,
        second_gain_grad,
        second_shift_grad,
    ) = lax.psum(
        (
            qkv_grad,
            qv_bias_grad,
            out_weight_grad,
            out_bias_grad,
            first_gain_grad,
            first_shift_grad,
            down_weight_grad,
            down_bias_grad,
            up_weight_grad,
            up_bias_grad,
            second_gain_grad,
            second_shift_grad,
        ),
        "seq",
    )
    norm_gains_grad = jnp.stack([first_gain_grad, second_gain_grad])
    norm_shifts_grad = jnp.stack([first_shift_grad, second_shift_grad])
    return (
        out_rows,
        rows_grad,
        norm_gains_grad,
        norm_shifts_grad,
        qkv_grad,
        qv_bias_grad,
        out_weight_grad,
        out_bias_grad,
        up_weight_grad,
        up_bias_grad,
        down_weight_grad,
        down_bias_grad,
    )


def solution(mesh):
    placed = (
        P("seq", None),
        P(),
        P(),
        P(),
        P(None, None, "head"),
        P(None, "head"),
        P("head", None),
        P(),
        P(None, "head"),
        P("head"),
        P("head", None),
        P(),
        P("seq", None),
    )
    return jax.shard_map(
        local,
        mesh=mesh,
        in_specs=placed,
        out_specs=(
            P("seq", None),
            P("seq", None),
            P(),
            P(),
            P(None, None, "head"),
            P(None, "head"),
            P("head", None),
            P(),
            P(None, "head"),
            P("head"),
            P("head", None),
            P(),
        ),
        check_vma=False,
    )
```

profile of v0, /device:TPU:0, one launch (start us, length us, event | category | flops | bytes accessed | tf_op | source)
XLA Modules:
  0.0 1449.7 jit_solution(5356410478210324382)
XLA Ops:
  42.2 6.9 fusion.232
  61.7 7.3 fusion.228
  124.2 7.4 fusion.224
  150.6 48.8 %while.115 = (s32[]{:T(128)}, f32[8,1,1024,48]{2,3,1,0:T(8,128)}, f32[8,1,1024]{2,1,0:T(1,128)S(1)}, f32[8,1,1024]{2,1,0:T(1,128)S(1)}, f32[8,1,1024]{2,1,0:T(1,...) while((s32[]{:T(128)}, f32[8,1,1024,48]{2,3,1,0:T(8,128)}, ...), condition=%wide.region_5.6_spmd, body=%wide.region_2.5_spmd.sunk | while | flops 219201536 | bytes 13650029 | solution.py:153
  202.8 7.7 fusion.220
  324.4 40.4 %while.116 = (s32[]{:T(128)}, f32[8,1,512,48]{2,3,1,0:T(8,128)S(1)}, f32[8,1,512]{2,1,0:T(1,128)S(1)}, f32[8,1,1024]{2,1,0:T(1,128)}, f32[8,1,512]{2,1,0:T(1,128...) while((s32[]{:T(128)}, f32[8,1,512,48]{2,3,1,0:T(8,128)S(1)}, ...), condition=%wide.region_13.14_spmd, body=%wide.region_10.13_spmd.sunk | while | flops 105406464 | bytes 7086193 | solution.py:153
  386.1 18.7 %while.117 = (s32[]{:T(128)}, f32[4,2,256,48]{2,3,1,0:T(8,128)}, f32[4,2,256]{2,1,0:T(2,128)S(1)}, f32[4,2,1024]{2,1,0:T(2,128)}, f32[4,2,256]{2,1,0:T(2,128)}, ...) while((s32[]{:T(128)}, f32[4,2,256,48]{2,3,1,0:T(8,128)}, ...), condition=%wide.region_21.22_spmd, body=%wide.region_18.21_spmd.sunk | while | flops 105406464 | bytes 6881393 | solution.py:153
  425.6 8.5 while.118
  491.9 52.1 %all-reduce.8.cloned.1.call-done = bf16[1024,768]{1,0:T(8,128)(2,1)} async-done(((bf16[1024,768]{1,0:T(8,128)(2,1)}), bf16[1024,768]{1,0:T(8,128)(2,1)}) %all-reduce.8.cloned.1.call-update) | async-done | bytes 1572880 | tf_op jit(solution)/shard_map/psum | solution.py:342
  547.8 4.9 multiply_convert_fusion.4
  552.7 6.2 fusion.324
  595.5 6.9 convolution_convert_fusion.2
  602.4 13.6 all-reduce.10.cloned.1.call-done
  661.9 112.6 %while.119 = (s32[]{:T(128)}, f32[8,1,1024,48]{2,3,1,0:T(8,128)}, f32[8,1,1024,48]{2,3,1,0:T(8,128)}, f32[8,1,1024,48]{2,3,1,0:T(8,128)}, f32[8,1,1024]{2,1,0:T(...) while((s32[]{:T(128)}, f32[8,1,1024,48]{2,3,1,0:T(8,128)}, ...), condition=%wide.region_47.48_spmd, body=%wide.region_46.47_spmd.sunk | while | flops 518095872 | bytes 21038224 | solution.py:153
  801.1 11.4 while.122
  822.2 27.2 %while.121 = (s32[]{:T(128)}, f32[4,2,256,48]{2,3,1,0:T(8,128)S(1)}, f32[4,2,1024,48]{2,3,1,0:T(8,128)}, f32[4,2,1024,48]{2,3,1,0:T(8,128)}, f32[4,2,1024]{2,1,0...) while((s32[]{:T(128)}, f32[4,2,256,48]{2,3,1,0:T(8,128)S(1)}, ...), condition=%wide.region_57.58_spmd, body=%wide.region_56.57_spmd.sunk | while | flops 256500224 | bytes 11156625 | solution.py:153
  855.0 76.0 %while.120 = (s32[]{:T(128)}, f32[8,1,512,48]{2,3,1,0:T(8,128)S(1)}, f32[8,1,1024,48]{2,3,1,0:T(8,128)}, f32[8,1,1024,48]{2,3,1,0:T(8,128)}, f32[8,1,1024]{2,1,0...) while((s32[]{:T(128)}, f32[8,1,512,48]{2,3,1,0:T(8,128)S(1)}, ...), condition=%wide.region_52.53_spmd, body=%wide.region_51.52_spmd.sunk | while | flops 256451072 | bytes 11275409 | solution.py:153
  951.4 4.8 mul.1120
  965.4 4.7 mul.1139
  980.9 4.7 mul.1157
  987.9 4.7 mul.1144
  1019.5 5.0 mul.1160
  1062.8 10.0 add_convert_fusion.14
  1077.2 7.4 fusion.325
  1084.7 4.9 fusion.245
  1126.6 7.5 fusion.244
  1134.2 28.0 %all-reduce.14.cloned.1.call-done = (bf16[1024,768]{1,0:T(8,128)(2,1)}, bf16[1024,768]{1,0:T(8,128)(2,1)}) async-done(((bf16[1024,768]{1,0:T(8,128)(2,1)}, bf16[1024,768]{1,0:T(8,128)(2,1)}), (bf16[1024,768]{1,0:T(8,128)(2,1)}, bf16[1024,768]{1,0:T(8,128)(2,1)})) %all-reduce.14.cloned.1.call-update) | async-done | bytes 3145744 | tf_op jit(solution)/shard_map/psum | solution.py:356
  1165.2 64.8 %all-reduce = (f32[1,768]{1,0:T(1,128)S(1)}, f32[1,768]{1,0:T(1,128)S(1)}, f32[1,768]{1,0:T(1,128)S(1)}, f32[1,768]{1,0:T(1,128)S(1)}, f32[2,384]{1,0:T(2,128)},...) all-reduce(f32[1,768]{1,0:T(1,128)S(1)} %stack.46, ...), channel_id=1, replica_groups=mesh['seq'=16,'head'=2] {'seq'}, use_global_device_ids=true, to_apply=%region_72.73 | all-reduce | flops 6912 | bytes 55296 | tf_op jit(solution)/shard_map/psum | solution.py:448
  1231.2 5.6 fusion.207
  1236.9 190.9 %all-reduce.12.cloned.1.call-done = (f32[3,768,384]{1,2,0:T(8,128)}, f32[384,768]{1,0:T(8,128)}, f32[768,1536]{1,0:T(8,128)}, f32[1536,768]{1,0:T(8,128)}) async-done(((f32[3,768,384]{1,2,0:T(8,128)}, f32[384,768]{1,0:T(8,128)}, f32[768,1536]{1,0:T(8,128)}, f32[1536,768]{1,0:T(8,128)}), (f32[3,768,384]{1,2,0:T(8,128)}, f32[384,768]{1,0:T(8,128)}, f32[768,1536]{1,0:T(8,128)}, ...) | async-done | bytes 14155792 | tf_op jit(solution)/shard_map/psum | solution.py:448
  1427.8 5.2 copy.897
  1434.1 5.5 copy.1042
  (1229 shorter events, 963.7 us)
Async XLA Ops:
  7.2 536.8 %all-reduce.8.cloned.1.call-start = ((), (), s32[]{:S(2)}) async-start(), calls=%async_computation | async-start | bytes 3145728 | tf_op jit(solution)/shard_map/psum | solution.py:342
  9.5 217.9 %collective-permute-start.18 = (bf16[8,64]{1,0:T(8,128)(2,1)}, bf16[8,64]{1,0:T(8,128)(2,1)}, u32[]{:S(2)}, u32[]{:S(2)}) collective-permute-start(bf16[8,64]{1,0:T(8,128)(2,1)} %get-tuple-element.1174), channel_id=1, source_target_pairs={{0,2},{2,0},{4,6},{6,4},{8,10},{10,8},{12,14},{14,12},{16,18},{18,... | collective-permute-start | bytes 3080 | tf_op jit(solution)/shard_map/ppermute | solution.py:34
  12.2 220.6 %collective-permute-start.3 = (bf16[8,256]{1,0:T(8,128)(2,1)}, bf16[8,256]{1,0:T(8,128)(2,1)}, u32[]{:S(2)}, u32[]{:S(2)}) collective-permute-start(bf16[8,256]{1,0:T(8,128)(2,1)} %bitcast_convert_fusion.3), channel_id=1, source_target_pairs={{0,2},{2,0},{4,6},{6,4},{8,10},{10,8},{12,14},{14,12},{16,18},{18,... | collective-permute-start | bytes 12296 | tf_op jit(solution)/shard_map/ppermute | solution.py:34
  49.1 205.8 %collective-permute-start.22 = (bf16[8,64,48]{2,0,1:T(8,128)(2,1)}, bf16[8,64,48]{2,0,1:T(8,128)(2,1)}, u32[]{:S(2)}, u32[]{:S(2)}) collective-permute-start(bf16[8,64,48]{2,0,1:T(8,128)(2,1)} %bitcast.144), channel_id=1, source_target_pairs={{0,2},{2,0},{4,6},{6,4},{8,10},{10,8},{12,14},{14,12},{16,18},{18,... | collective-permute-start | bytes 147464 | tf_op jit(solution)/shard_map/ppermute | solution.py:34
  49.5 209.3 %collective-permute-start.26 = (bf16[8,64,48]{2,0,1:T(8,128)(2,1)S(1)}, bf16[8,64,48]{2,0,1:T(8,128)(2,1)}, u32[]{:S(2)}, u32[]{:S(2)}) collective-permute-start(bf16[8,64,48]{2,0,1:T(8,128)(2,1)S(1)} %bitcast.891), channel_id=1, source_target_pairs={{0,2},{2,0},{4,6},{6,4},{8,10},{10,8},{12,14},{14,12},{16,18},{18,... | collective-permute-start | bytes 147464 | tf_op jit(solution)/shard_map/ppermute | solution.py:34
  69.0 192.6 %collective-permute-start.15 = (bf16[8,128,48]{2,0,1:T(8,128)(2,1)}, bf16[8,128,48]{2,0,1:T(8,128)(2,1)}, u32[]{:S(2)}, u32[]{:S(2)}) collective-permute-start(bf16[8,128,48]{2,0,1:T(8,128)(2,1)} %bitcast.133), channel_id=1, source_target_pairs={{0,2},{2,0},{4,6},{6,4},{8,10},{10,8},{12,14},{14,12},{16,18},{18,... | collective-permute-start | bytes 294920 | tf_op jit(solution)/shard_map/ppermute | solution.py:34
  232.8 31.1 %collective-permute-start.12 = (bf16[8,128,48]{2,0,1:T(8,128)(2,1)}, bf16[8,128,48]{2,0,1:T(8,128)(2,1)}, u32[]{:S(2)}, u32[]{:S(2)}) collective-permute-start(bf16[8,128,48]{2,0,1:T(8,128)(2,1)} %bitcast.867), channel_id=1, source_target_pairs={{0,2},{2,0},{4,6},{6,4},{8,10},{10,8},{12,14},{14,12},{16,18},{18,... | collective-permute-start | bytes 294920 | tf_op jit(solution)/shard_map/ppermute | solution.py:34
  254.2 30.5 %collective-permute-start.7 = (bf16[8,256,48]{2,0,1:T(8,128)(2,1)}, bf16[8,256,48]{2,0,1:T(8,128)(2,1)S(1)}, u32[]{:S(2)}, u32[]{:S(2)}) collective-permute-start(bf16[8,256,48]{2,0,1:T(8,128)(2,1)} %bitcast.841), channel_id=1, source_target_pairs={{0,2},{2,0},{4,6},{6,4},{8,10},{10,8},{12,14},{14,12},{16,18},{18,... | collective-permute-start | bytes 589832 | tf_op jit(solution)/shard_map/ppermute | solution.py:34
  254.9 32.3 %collective-permute-start.5 = (bf16[8,256,48]{2,0,1:T(8,128)(2,1)}, bf16[8,256,48]{2,0,1:T(8,128)(2,1)S(1)}, u32[]{:S(2)}, u32[]{:S(2)}) collective-permute-start(bf16[8,256,48]{2,0,1:T(8,128)(2,1)} %bitcast.838), channel_id=1, source_target_pairs={{0,2},{2,0},{4,6},{6,4},{8,10},{10,8},{12,14},{14,12},{16,18},{18,... | collective-permute-start | bytes 589832 | tf_op jit(solution)/shard_map/ppermute | solution.py:34
  258.8 59.7 %collective-permute-start.2 = (bf16[8,512,48]{1,2,0:T(8,128)(2,1)}, bf16[8,512,48]{1,2,0:T(8,128)(2,1)}, u32[]{:S(2)}, u32[]{:S(2)}) collective-permute-start(bf16[8,512,48]{1,2,0:T(8,128)(2,1)} %copy.730), channel_id=1, source_target_pairs={{0,2},{2,0},{4,6},{6,4},{8,10},{10,8},{12,14},{14,12},{16,18},{18,... | collective-permute-start | bytes 1179656 | tf_op jit(solution)/shard_map/ppermute | solution.py:34
  261.6 53.3 %collective-permute-start.1 = (bf16[8,512,48]{1,2,0:T(8,128)(2,1)}, bf16[8,512,48]{1,2,0:T(8,128)(2,1)}, u32[]{:S(2)}, u32[]{:S(2)}) collective-permute-start(bf16[8,512,48]{1,2,0:T(8,128)(2,1)} %copy.724), channel_id=1, source_target_pairs={{0,2},{2,0},{4,6},{6,4},{8,10},{10,8},{12,14},{14,12},{16,18},{18,... | collective-permute-start | bytes 1179656 | tf_op jit(solution)/shard_map/ppermute | solution.py:34
  287.2 22.1 %collective-permute-start.28 = (bf16[8,256,48]{1,2,0:T(8,128)(2,1)}, bf16[8,256,48]{1,2,0:T(8,128)(2,1)}, u32[]{:S(2)}, u32[]{:S(2)}) collective-permute-start(bf16[8,256,48]{1,2,0:T(8,128)(2,1)} %maximum_select_fusion.23), channel_id=1, source_target_pairs={{0,8},{8,0},{2,10},{10,2},{4,12},{12,4},{6,14},{14,6},{16,24},{24,... | collective-permute-start | bytes 589832 | tf_op jit(solution)/shard_map/ppermute | solution.py:34
  302.8 78.5 %collective-permute-start.8 = (bf16[8,512,48]{1,2,0:T(8,128)(2,1)}, bf16[8,512,48]{1,2,0:T(8,128)(2,1)}, u32[]{:S(2)}, u32[]{:S(2)}) collective-permute-start(bf16[8,512,48]{1,2,0:T(8,128)(2,1)} %maximum_select_fusion.10), channel_id=1, source_target_pairs={{0,4},{4,0},{2,6},{6,2},{8,12},{12,8},{10,14},{14,10},{16,20},{20,... | collective-permute-start | bytes 1179656 | tf_op jit(solution)/shard_map/ppermute | solution.py:34
  309.3 73.7 %collective-permute-start.6 = (bf16[8,512,48]{1,2,0:T(8,128)(2,1)}, bf16[8,512,48]{1,2,0:T(8,128)(2,1)}, u32[]{:S(2)}, u32[]{:S(2)}) collective-permute-start(bf16[8,512,48]{1,2,0:T(8,128)(2,1)} %maximum_select_fusion.8), channel_id=1, source_target_pairs={{0,4},{4,0},{2,6},{6,2},{8,12},{12,8},{10,14},{14,10},{16,20},{20,... | collective-permute-start | bytes 1179656 | tf_op jit(solution)/shard_map/ppermute | solution.py:34
  312.5 108.8 %collective-permute-start.14 = (bf16[8,512,48]{1,2,0:T(8,128)(2,1)}, bf16[8,512,48]{1,2,0:T(8,128)(2,1)}, u32[]{:S(2)}, u32[]{:S(2)}) collective-permute-start(bf16[8,512,48]{1,2,0:T(8,128)(2,1)} %maximum_select_fusion.12), channel_id=1, source_target_pairs={{0,8},{8,0},{2,10},{10,2},{4,12},{12,4},{6,14},{14,6},{16,24},{24,... | collective-permute-start | bytes 1179656 | tf_op jit(solution)/shard_map/ppermute | solution.py:34
  314.9 108.7 %collective-permute-start.17 = (bf16[8,512,48]{1,2,0:T(8,128)(2,1)}, bf16[8,512,48]{1,2,0:T(8,128)(2,1)}, u32[]{:S(2)}, u32[]{:S(2)}) collective-permute-start(bf16[8,512,48]{1,2,0:T(8,128)(2,1)} %maximum_select_fusion.14), channel_id=1, source_target_pairs={{0,8},{8,0},{2,10},{10,2},{4,12},{12,4},{6,14},{14,6},{16,24},{24,... | collective-permute-start | bytes 1179656 | tf_op jit(solution)/shard_map/ppermute | solution.py:34
  318.6 135.6 %collective-permute-start.25 = (bf16[8,512,48]{1,2,0:T(8,128)(2,1)}, bf16[8,512,48]{1,2,0:T(8,128)(2,1)}, u32[]{:S(2)}, u32[]{:S(2)}) collective-permute-start(bf16[8,512,48]{1,2,0:T(8,128)(2,1)} %maximum_select_fusion.16), channel_id=1, source_target_pairs={{0,16},{16,0},{2,18},{18,2},{4,20},{20,4},{6,22},{22,6},{8,24},{24... | collective-permute-start | bytes 1179656 | tf_op jit(solution)/shard_map/ppermute | solution.py:34
  381.3 81.5 %collective-permute-start.29 = (bf16[8,512,48]{1,2,0:T(8,128)(2,1)}, bf16[8,512,48]{1,2,0:T(8,128)(2,1)}, u32[]{:S(2)}, u32[]{:S(2)}) collective-permute-start(bf16[8,512,48]{1,2,0:T(8,128)(2,1)} %maximum_select_fusion.17), channel_id=1, source_target_pairs={{0,16},{16,0},{2,18},{18,2},{4,20},{20,4},{6,22},{22,6},{8,24},{24... | collective-permute-start | bytes 1179656 | tf_op jit(solution)/shard_map/ppermute | solution.py:34
  491.9 124.2 %all-reduce.10.cloned.1.call-start = ((), (), s32[]{:S(2)}) async-start(), calls=%async_computation.1 | async-start | bytes 3145728 | tf_op jit(solution)/shard_map/psum | solution.py:377
  564.4 597.9 %all-reduce.14.cloned.1.call-start = ((), (), s32[]{:S(2)}) async-start(), calls=%async_computation.3 | async-start | bytes 6291456 | tf_op jit(solution)/shard_map/psum | solution.py:356
  790.2 202.4 %collective-permute-start.46 = (bf16[8,512,48]{1,2,0:T(8,128)(2,1)}, bf16[8,512,48]{1,2,0:T(8,128)(2,1)}, u32[]{:S(2)}, u32[]{:S(2)}) collective-permute-start(bf16[8,512,48]{1,2,0:T(8,128)(2,1)} %select_convert_fusion), channel_id=1, source_target_pairs={{0,16},{16,0},{2,18},{18,2},{4,20},{20,4},{6,22},{22,6},{8,24},{24... | collective-permute-start | bytes 1179656 | tf_op jit(solution)/shard_map/ppermute | solution.py:34
  797.3 197.2 %collective-permute-start.36 = (bf16[8,512,48]{1,2,0:T(8,128)(2,1)}, bf16[8,512,48]{1,2,0:T(8,128)(2,1)}, u32[]{:S(2)}, u32[]{:S(2)}) collective-permute-start(bf16[8,512,48]{1,2,0:T(8,128)(2,1)} %select_convert_fusion.4), channel_id=1, source_target_pairs={{0,16},{16,0},{2,18},{18,2},{4,20},{20,4},{6,22},{22,6},{8,24},{24... | collective-permute-start | bytes 1179656 | tf_op jit(solution)/shard_map/ppermute | solution.py:34
  817.9 179.5 %collective-permute-start.33 = (bf16[8,512,48]{1,2,0:T(8,128)(2,1)}, bf16[8,512,48]{1,2,0:T(8,128)(2,1)}, u32[]{:S(2)}, u32[]{:S(2)}) collective-permute-start(bf16[8,512,48]{1,2,0:T(8,128)(2,1)} %select_convert_fusion.5), channel_id=1, source_target_pairs={{0,8},{8,0},{2,10},{10,2},{4,12},{12,4},{6,14},{14,6},{16,24},{24,... | collective-permute-start | bytes 1179656 | tf_op jit(solution)/shard_map/ppermute | solution.py:34
  935.7 38.2 %collective-permute-start.30 = (bf16[8,512,48]{1,2,0:T(8,128)(2,1)}, bf16[8,512,48]{1,2,0:T(8,128)(2,1)}, u32[]{:S(2)}, u32[]{:S(2)}) collective-permute-start(bf16[8,512,48]{1,2,0:T(8,128)(2,1)} %select_convert_fusion.7), channel_id=1, source_target_pairs={{0,2},{2,0},{4,6},{6,4},{8,10},{10,8},{12,14},{14,12},{16,18},{18,... | collective-permute-start | bytes 1179656 | tf_op jit(solution)/shard_map/ppermute | solution.py:34
  935.7 34.5 %collective-permute-start.40 = (bf16[8,512,48]{1,2,0:T(8,128)(2,1)}, bf16[8,512,48]{1,2,0:T(8,128)(2,1)}, u32[]{:S(2)}, u32[]{:S(2)}) collective-permute-start(bf16[8,512,48]{1,2,0:T(8,128)(2,1)} %select_convert_fusion.3), channel_id=1, source_target_pairs={{0,2},{2,0},{4,6},{6,4},{8,10},{10,8},{12,14},{14,12},{16,18},{18,... | collective-permute-start | bytes 1179656 | tf_op jit(solution)/shard_map/ppermute | solution.py:34
  970.2 29.0 %collective-permute-start.43 = (bf16[8,512,48]{1,2,0:T(8,128)(2,1)S(1)}, bf16[8,512,48]{1,2,0:T(8,128)(2,1)}, u32[]{:S(2)}, u32[]{:S(2)}) collective-permute-start(bf16[8,512,48]{1,2,0:T(8,128)(2,1)S(1)} %copy-done.109), channel_id=1, source_target_pairs={{0,8},{8,0},{2,10},{10,2},{4,12},{12,4},{6,14},{14,6},{16,24},{24,... | collective-permute-start | bytes 1179656 | tf_op jit(solution)/shard_map/ppermute | solution.py:34
  973.9 28.1 %collective-permute-start.31 = (bf16[8,512,48]{1,2,0:T(8,128)(2,1)}, bf16[8,512,48]{1,2,0:T(8,128)(2,1)}, u32[]{:S(2)}, u32[]{:S(2)}) collective-permute-start(bf16[8,512,48]{1,2,0:T(8,128)(2,1)} %select_convert_fusion.6), channel_id=1, source_target_pairs={{0,4},{4,0},{2,6},{6,2},{8,12},{12,8},{10,14},{14,10},{16,20},{20,... | collective-permute-start | bytes 1179656 | tf_op jit(solution)/shard_map/ppermute | solution.py:34
  1006.3 25.1 %collective-permute-start.48 = (bf16[8,128,48]{1,2,0:T(8,128)(2,1)}, bf16[8,128,48]{1,2,0:T(8,128)(2,1)S(1)}, u32[]{:S(2)}, u32[]{:S(2)}) collective-permute-start(bf16[8,128,48]{1,2,0:T(8,128)(2,1)} %select_convert_fusion.15), channel_id=1, source_target_pairs={{0,4},{4,0},{2,6},{6,2},{8,12},{12,8},{10,14},{14,10},{16,20},{20,... | collective-permute-start | bytes 294920 | tf_op jit(solution)/shard_map/ppermute | solution.py:34
  1008.9 22.6 %collective-permute-start.38 = (bf16[8,128,48]{1,2,0:T(8,128)(2,1)}, bf16[8,128,48]{1,2,0:T(8,128)(2,1)S(1)}, u32[]{:S(2)}, u32[]{:S(2)}) collective-permute-start(bf16[8,128,48]{1,2,0:T(8,128)(2,1)} %select_convert_fusion.18), channel_id=1, source_target_pairs={{0,4},{4,0},{2,6},{6,2},{8,12},{12,8},{10,14},{14,10},{16,20},{20,... | collective-permute-start | bytes 294920 | tf_op jit(solution)/shard_map/ppermute | solution.py:34
  1013.2 19.1 %collective-permute-start.35 = (bf16[8,128,48]{1,2,0:T(8,128)(2,1)}, bf16[8,128,48]{1,2,0:T(8,128)(2,1)}, u32[]{:S(2)}, u32[]{:S(2)}) collective-permute-start(bf16[8,128,48]{1,2,0:T(8,128)(2,1)} %select_convert_fusion.19), channel_id=1, source_target_pairs={{0,2},{2,0},{4,6},{6,4},{8,10},{10,8},{12,14},{14,12},{16,18},{18,... | collective-permute-start | bytes 294920 | tf_op jit(solution)/shard_map/ppermute | solution.py:34
  1014.0 19.2 %collective-permute-start.45 = (bf16[8,128,48]{1,2,0:T(8,128)(2,1)}, bf16[8,128,48]{1,2,0:T(8,128)(2,1)}, u32[]{:S(2)}, u32[]{:S(2)}) collective-permute-start(bf16[8,128,48]{1,2,0:T(8,128)(2,1)} %select_convert_fusion.16), channel_id=1, source_target_pairs={{0,2},{2,0},{4,6},{6,4},{8,10},{10,8},{12,14},{14,12},{16,18},{18,... | collective-permute-start | bytes 294920 | tf_op jit(solution)/shard_map/ppermute | solution.py:34
  1077.2 350.6 %all-reduce.12.cloned.1.call-start = ((), (), s32[]{:S(2)}) async-start(), calls=%async_computation.2 | async-start | bytes 28311552 | tf_op jit(solution)/shard_map/psum | solution.py:448
  (227 other events, 2001.7 us)
Sparse Core Ops, SparseCore 0:
  492.0 51.9 all-reduce.7
  564.5 51.4 all-reduce.9
  1077.2 85.0 all-reduce.13
  1168.5 259.2 all-reduce.11
where the time goes:
time: 1470 us; the launch traced here: 1450 us
  local copies, waits for them, and re-layouts  457 us (31%)
  matrix products  321 us (22%)
  waiting for transfers between devices  302 us (21%)
  other arithmetic  242 us (16%)
  blocking collectives  64.8 us (4%)
  starting transfers between devices  42.7 us (3%)
  between operations  17.2 us (1%)
    psum x1, waiting for transfers between devices, local(): lax.psum((qkv_grad, qv_bias_grad, out_weight_grad, out_bias_grad, first_g...  191 us
    mul x54, local copies, waits for them, and re-layouts, place_rows(): spread = moved_rows[:, None] * select_mask  153 us
    dot_general x45, matrix products, masked_scores(): jnp.einsum('egy,ehy->egh', query_rows, key_matrix, preferred_element_type...  72.4 us
    psum x1, blocking collectives, local(): lax.psum((qkv_grad, qv_bias_grad, out_weight_grad, out_bias_grad, first_g...  64.8 us
    psum x1, waiting for transfers between devices, local(): lax.psum(jnp.dot(merged_low, out_weight, preferred_element_type=jnp.float...  52.1 us
    reduce_sum x16, other arithmetic, select_rows(): chosen = jnp.sum(folded * select_mask, axis=1)  46.8 us
    select_n x33, other arithmetic, join_halves(): jnp.where(is_upper, jnp.concatenate([peer_piece, own_piece], 1), jnp.conc...  45.5 us
    dot_general x23, matrix products, attend(): jnp.einsum('efw,ews->efs', weight_matrix.astype(jnp.bfloat16), value_rows...  44.6 us
  transfers between devices with their start and end apart: 54, of which 15 were waited for; matrix products, arithmetic and copies ran while one was open for 51% of the time, Pallas kernels for 0%

commit v1 on v0

v1 whole, which is shorter than its diff:
```python
import functools
import math

import jax
import jax.numpy as jnp
import numpy as np
from jax import lax
from jax.experimental import pallas as pl
from jax.experimental.pallas import tpu as pltpu
from jax.sharding import PartitionSpec as P

HD = 48
SEG = 1024
LANES = 128
LEVELS = 5
FOLD = 16

EPS = 1e-05
ROOT = math.sqrt(HD)
EXP_SCALE = math.log2(math.e) / ROOT
ROOT_HALF = 1.0 / math.sqrt(2.0)
DENSITY_NORM = 1.0 / math.sqrt(2.0 * math.pi)
ABSENT = -1e20

ONE = 96
MASK = 99
MULT = 100
TOP = 127

ORDER = (0, 8, 4, 12, 2, 6, 10, 14, 1, 3, 5, 7, 9, 11, 13, 15)
CLASS = (4, 3, 2, 2, 1, 1, 1, 1, 0, 0, 0, 0, 0, 0, 0, 0)

F32 = jnp.float32
BF16 = jnp.bfloat16


def params(mib=48):
    return pltpu.CompilerParams(vmem_limit_bytes=mib * 2**20)


def dot(left, right):
    return jnp.dot(left, right, preferred_element_type=F32)


def dot_rt(left, right):
    return lax.dot_general(left, right, (((1,), (1,)), ((), ())), preferred_element_type=F32)


def dot_lt(left, right):
    return lax.dot_general(left, right, (((0,), (0,)), ((), ())), preferred_element_type=F32)


def full(shape):
    return pl.BlockSpec(shape, lambda *_: (0,) * len(shape))


def per_head(rows, lanes=LANES):
    return pl.BlockSpec((1, rows, lanes), lambda h: (h, 0, 0))


def shape(dims, kind):
    return jax.ShapeDtypeStruct(dims, kind)


def split3(x):
    high = x.astype(BF16).astype(F32)
    rest = x - high
    middle = rest.astype(BF16).astype(F32)
    return high, middle, rest - middle


def with_terms(block, lane, terms):
    high, middle, low = split3(terms)
    block = jnp.where(lane == ONE, high, block)
    block = jnp.where(lane == ONE + 1, middle, block)
    return jnp.where(lane == ONE + 2, low, block)


def unit_rows(x):
    mean = jnp.mean(x, -1, keepdims=True)
    centred = x - mean
    inverse = lax.rsqrt(jnp.mean(centred * centred, -1, keepdims=True) + EPS)
    return centred * inverse, inverse


def norm_back(gradient, unit, inverse, gain):
    z = gradient * gain
    return inverse * (
        z - jnp.mean(z, -1, keepdims=True) - unit * jnp.mean(z * unit, -1, keepdims=True)
    )


def mult_table(level, blocks):
    table = np.zeros((len(blocks), LANES), np.float32)
    for row, key_class in enumerate(blocks):
        for j in range(level + 1, key_class + 1):
            value = np.float32(ROOT * math.log((j - level + 1) / (j - level)))
            high = np.float32(value.astype(jnp.bfloat16))
            table[row, MULT + j - 1] = high
            table[row, MULT + 4 + j - 1] = np.float32((value - high).astype(jnp.bfloat16))
    return table


def own_table():
    return mult_table(0, CLASS)


def peer_table():
    return np.concatenate(
        [
            mult_table(1, CLASS[:8]),
            mult_table(2, CLASS[:4] * 2),
            mult_table(3, CLASS[:2] * 4),
            mult_table(4, CLASS[:1] * 8),
        ]
    )


def project_kernel(
    place, rows, gain, shift, w, bias, table, q, kv, s1, sx, sz1, sz, normed, wide, w_tmp, b_tmp, q_tmp, kv_tmp
):
    h = pl.program_id(0)
    n, d = rows.shape
    heads = w.shape[2] // HD
    block = n // FOLD

    @pl.when(h == 0)
    def _():
        unit, _ = unit_rows(rows[...].astype(F32))
        normed[...] = (unit * gain[...] + shift[...]).astype(BF16)

    for k in range(heads):

        @pl.when(h == k)
        def _():
            cut = slice(k * HD, (k + 1) * HD)
            w_tmp[:, :LANES] = jnp.concatenate(
                [w[0, :, cut], jnp.zeros((d, LANES - HD), BF16)], axis=1
            )
            w_tmp[:, LANES:] = jnp.concatenate(
                [w[1, :, cut], w[2, :, cut], jnp.zeros((d, LANES - 2 * HD), BF16)], axis=1
            )
            b_tmp[:, :LANES] = jnp.concatenate(
                [bias[0:1, cut], jnp.zeros((1, LANES - HD), F32)], axis=1
            )
            b_tmp[:, LANES:] = jnp.concatenate(
                [
                    jnp.zeros((1, HD), F32),
                    bias[1:2, cut],
                    jnp.ones((1, 3), F32),
                    jnp.zeros((1, LANES - 2 * HD - 3), F32),
                ],
                axis=1,
            )

    wide[0] = w_tmp[...]
    product = dot(normed[...], w_tmp[...]) + b_tmp[...]
    q_tmp[...] = product[:, :LANES]
    kv_tmp[...] = product[:, LANES:]
    lane = lax.broadcasted_iota(jnp.int32, (block, LANES), 1)
    step = lax.broadcasted_iota(jnp.int32, (block, LANES), 0) * FOLD
    head = place[0] + h
    for p in range(FOLD):
        c = (head + ORDER[p]) % FOLD
        here = step + c < place[1]
        at = pl.ds(p * block, block)
        q_rows = q_tmp[pl.ds(c, block, stride=FOLD), :]
        kv_rows = kv_tmp[pl.ds(c, block, stride=FOLD), :]
        level = CLASS[p]
        flags = ((lane >= MULT) & (lane < MULT + level)) | (
            (lane >= MULT + 4) & (lane < MULT + 4 + level)
        )
        q_rows = jnp.where(flags, 1.0, q_rows)
        q_rows = jnp.where(lane == MASK, jnp.where(here, 1.0, 0.0), q_rows)
        q[0, at, :] = q_rows.astype(BF16)
        kv_rows = jnp.where(lane == MASK, jnp.where(here, 0.0, ABSENT), kv_rows)
        kv[0, at, :] = (kv_rows + table[p : p + 1, :]).astype(BF16)
        if level >= 1:
            low = kv_rows.astype(BF16)
            s1[0, at, :] = low
            if level >= 2:
                sx[0, at, :] = low
            if level >= 3:
                sz1[0, at, :] = low
            if level >= 4:
                sz[0, at, :] = low


def project(place, rows, gain, shift, w, bias):
    n, d = rows.shape
    heads = w.shape[2] // HD
    table = jnp.asarray(own_table())
    sizes = (n, n, n // 2, n // 4, n // 8, n // 16)
    return pl.pallas_call(
        project_kernel,
        grid=(heads,),
        in_specs=[
            pl.BlockSpec(memory_space=pltpu.SMEM),
            full(rows.shape),
            full(gain.shape),
            full(shift.shape),
            full(w.shape),
            full(bias.shape),
            full(table.shape),
        ],
        out_specs=[per_head(m) for m in sizes]
        + [full((n, d)), pl.BlockSpec((1, d, 2 * LANES), lambda h: (h, 0, 0))],
        out_shape=[shape((heads, m, LANES), BF16) for m in sizes]
        + [shape((n, d), BF16), shape((heads, d, 2 * LANES), BF16)],
        scratch_shapes=[
            pltpu.VMEM((d, 2 * LANES), BF16),
            pltpu.VMEM((1, 2 * LANES), F32),
            pltpu.VMEM((n, LANES), F32),
            pltpu.VMEM((n, LANES), F32),
        ],
        compiler_params=params(),
        cost_estimate=pl.CostEstimate(
            flops=2 * n * d * heads * 256, bytes_accessed=14 * 2**20, transcendentals=0
        ),
        name="project",
    )(place, rows, gain, shift, w, bias, table)


def own_kernel(q, kv, out, *, block):
    n = q.shape[1]
    keys = kv[0]
    lane = lax.broadcasted_iota(jnp.int32, (block, LANES), 1)

    def scores(i):
        return dot_rt(q[0, pl.ds(i * block, block), :], keys)

    now = scores(0)
    for i in range(n // block):
        later = scores(i + 1) if (i + 1) * block < n else None
        top = jnp.max(now, -1, keepdims=True)
        weights = jnp.exp2((now - top) * EXP_SCALE).astype(BF16)
        out[0, pl.ds(i * block, block), :] = jnp.where(lane == TOP, top, dot(weights, keys))
        now = later


def own_attention(q, kv):
    heads, n, _ = q.shape
    return pl.pallas_call(
        functools.partial(own_kernel, block=256),
        grid=(heads,),
        in_specs=[per_head(n)] * 2,
        out_specs=per_head(n),
        out_shape=shape((heads, n, LANES), F32),
        compiler_params=params(),
        cost_estimate=pl.CostEstimate(
            flops=heads * n * n * 1024, bytes_accessed=8 * 2**20, transcendentals=heads * n * n
        ),
        name="own_attention",
    )(q, kv)


def peers_kernel(
    place, q, own, cs1, rx, crx, zc, rx2, czc, crx2, table, pick, merged, kv_all, qb, low, nat, wide
):
    h = pl.program_id(0)
    n = q.shape[1]
    block = n // FOLD
    at = 0
    near = (zc, rx2, czc, crx2)
    pieces = [(cs1, 0, n // 2), (rx, 0, n // 4), (crx, 0, n // 4)]
    pieces += [(r, 0, n // 8) for r in near] + [(r, n // 8, n // 8) for r in near]
    for ref, start, count in pieces:
        for k in range(count // block):
            rows = ref[0, pl.ds(start + k * block, block), :].astype(F32)
            index = at // block
            kv_all[0, pl.ds(at, block), :] = (rows + table[index : index + 1, :]).astype(BF16)
            at += block

    head = place[0] + h
    chunks = [
        (0, n // 16, 2 * n),
        (n // 16, n // 16, 3 * n // 2),
        (n // 8, n // 8, n),
        (n // 4, n // 4, n // 2),
        (n // 2, n // 2, 0),
    ]
    scores = []
    for start, count, keys in chunks:
        if keys:
            scores.append(dot_rt(q[0, pl.ds(start, count), :], kv_all[0, pl.ds(0, keys), :]))
        else:
            scores.append(None)
    for (start, count, keys), s in zip(chunks, scores):
        rows = pl.ds(start, count)
        lane = lax.broadcasted_iota(jnp.int32, (count, LANES), 1)
        o = own[0, rows, :]
        top = o[:, TOP : TOP + 1]
        if keys:
            new = jnp.maximum(top, jnp.max(s, -1, keepdims=True))
            weights = jnp.exp2((s - new) * EXP_SCALE).astype(BF16)
            o = o * jnp.exp2((top - new) * EXP_SCALE) + dot(weights, kv_all[0, pl.ds(0, keys), :])
            top = new
        total = o[:, ONE : ONE + 1]
        o = jnp.where((lane >= HD) & (lane < 2 * HD), o / total, 0.0)
        merged[0, rows, :] = o
        lse = top + jnp.log2(total) * (1.0 / EXP_SCALE)
        qb[0, rows, :] = with_terms(q[0, rows, :].astype(F32), lane, -lse).astype(BF16)
        for p in range(start // block, (start + count) // block):
            c = (head + ORDER[p]) % FOLD
            off = p * block - start
            nat[pl.ds(c, block, stride=FOLD), :] = o[off : off + block]
    wide[:, pl.ds(pl.multiple_of(h * LANES, LANES), LANES)] = nat[...].astype(BF16)

    @pl.when(h == pl.num_programs(0) - 1)
    def _():
        low[...] = dot(wide[...], pick[...]).astype(BF16)


def pick_values(heads):
    m = np.zeros((heads * LANES, heads * HD), np.float32)
    for h in range(heads):
        for j in range(HD):
            m[h * LANES + HD + j, h * HD + j] = 1.0
    return m


def peers_attention(place, q, own, received):
    heads, n, _ = q.shape
    table = jnp.asarray(peer_table())
    pick = jnp.asarray(pick_values(heads), BF16)
    return pl.pallas_call(
        peers_kernel,
        grid=(heads,),
        in_specs=[pl.BlockSpec(memory_space=pltpu.SMEM), per_head(n), per_head(n)]
        + [per_head(r.shape[1]) for r in received]
        + [full(table.shape), full(pick.shape)],
        out_specs=[per_head(n), per_head(2 * n), per_head(n), full((n, heads * HD))],
        out_shape=[
            shape((heads, n, LANES), F32),
            shape((heads, 2 * n, LANES), BF16),
            shape((heads, n, LANES), BF16),
            shape((n, heads * HD), BF16),
        ],
        scratch_shapes=[pltpu.VMEM((n, LANES), F32), pltpu.VMEM((n, heads * LANES), BF16)],
        compiler_params=params(),
        cost_estimate=pl.CostEstimate(
            flops=heads * n * n * 512, bytes_accessed=24 * 2**20, transcendentals=heads * n * n // 2
        ),
        name="peers_attention",
    )(place, q, own, *received, table, pick)


def feed_kernel(
    place, rows, cot, own_c, peer_c, own_w, peer_w, out_b, gain, shift, up_w, up_b, down_w,
    hidden, normed, act, grad_pre, grad_normed, up_b_grad, w_tmp,
):
    i = pl.program_id(0)
    half = own_w.shape[0]
    first = place[2] == 0

    @pl.when(i == 0)
    def _():
        w_tmp[:half] = jnp.where(first, own_w[...], peer_w[...])
        w_tmp[half:] = jnp.where(first, peer_w[...], own_w[...])

    one = jnp.where(first, own_c[...], peer_c[...])
    two = jnp.where(first, peer_c[...], own_c[...])
    attended = dot(one, w_tmp[:half]) + dot(two, w_tmp[half:])
    hid = rows[...].astype(F32) + (attended + out_b[...])
    hidden[...] = hid
    unit, _ = unit_rows(hid)
    low = (unit * gain[...] + shift[...]).astype(BF16)
    normed[...] = low
    pre = dot(low, up_w[...]) + up_b[...]
    phi = 0.5 * (1.0 + lax.erf(pre * ROOT_HALF))
    act[...] = (pre * phi).astype(BF16)
    slope = phi + pre * jnp.exp(-0.5 * pre * pre) * DENSITY_NORM
    gradient = dot_rt(cot[...], down_w[...]) * slope
    total = jnp.sum(gradient, 0, keepdims=True)

    @pl.when(i == 0)
    def _():
        up_b_grad[...] = total

    @pl.when(i > 0)
    def _():
        up_b_grad[...] += total

    gradient = gradient.astype(BF16)
    grad_pre[...] = gradient
    grad_normed[...] = dot_rt(gradient, up_w[...]).astype(BF16)


def feed(place, rows, cot, own_c, peer_c, own_w, peer_w, out_b, gain, shift, up_w, up_b, down_w):
    n, d = rows.shape
    block = 256
    ff = up_w.shape[1]
    half = own_w.shape[0]

    def part(lanes):
        return pl.BlockSpec((block, lanes), lambda i: (i, 0))

    return pl.pallas_call(
        feed_kernel,
        grid=(n // block,),
        in_specs=[
            pl.BlockSpec(memory_space=pltpu.SMEM),
            part(d),
            part(d),
            part(half),
            part(half),
            full(own_w.shape),
            full(peer_w.shape),
            full((1, d)),
            full((1, d)),
            full((1, d)),
            full(up_w.shape),
            full((1, ff)),
            full(down_w.shape),
        ],
        out_specs=[part(d), part(d), part(ff), part(ff), part(d), full((1, ff))],
        out_shape=[
            shape((n, d), F32),
            shape((n, d), BF16),
            shape((n, ff), BF16),
            shape((n, ff), BF16),
            shape((n, d), BF16),
            shape((1, ff), F32),
        ],
        scratch_shapes=[pltpu.VMEM((2 * half, d), BF16)],
        compiler_params=params(),
        cost_estimate=pl.CostEstimate(
            flops=2 * n * d * (ff * 3 + d), bytes_accessed=24 * 2**20, transcendentals=2 * n * ff
        ),
        name="feed_forward",
    )(place, rows, cot, own_c, peer_c, own_w, peer_w, out_b, gain, shift, up_w, up_b, down_w)


def turn_kernel(
    place, cot, own_g, peer_g, hidden, gain, out_w, merged, grad_hidden, low_out, do, sums, gm_tmp
):
    h = pl.program_id(0)
    n, d = cot.shape
    block = n // FOLD

    @pl.when(h == 0)
    def _():
        unit, inverse = unit_rows(hidden[...])
        gradient = own_g[...].astype(F32) + peer_g[...].astype(F32)
        outer = cot[...].astype(F32)
        total = outer + norm_back(gradient, unit, inverse, gain[...])
        grad_hidden[...] = total
        low_out[...] = total.astype(BF16)
        sums[0:1, :] = jnp.sum(gradient * unit, 0, keepdims=True)
        sums[1:2, :] = jnp.sum(gradient, 0, keepdims=True)
        sums[2:3, :] = jnp.sum(total, 0, keepdims=True)
        sums[3:4, :] = jnp.sum(outer, 0, keepdims=True)
        sums[4:8, :] = jnp.zeros((4, d), F32)

    gm_tmp[...] = dot_rt(low_out[...], out_w[0]).astype(BF16).astype(F32)
    lane = lax.broadcasted_iota(jnp.int32, (block, LANES), 1)
    head = place[0] + h
    for p in range(FOLD):
        c = (head + ORDER[p]) % FOLD
        at = pl.ds(p * block, block)
        gradient = gm_tmp[pl.ds(c, block, stride=FOLD), :]
        delta = jnp.sum(gradient * merged[0, at, :], -1, keepdims=True)
        do[0, at, :] = with_terms(gradient, lane, -delta).astype(BF16)


def turn(place, cot, own_g, peer_g, hidden, gain, out_w, merged):
    n, d = cot.shape
    heads = merged.shape[0]
    return pl.pallas_call(
        turn_kernel,
        grid=(heads,),
        in_specs=[
            pl.BlockSpec(memory_space=pltpu.SMEM),
            full((n, d)),
            full((n, d)),
            full((n, d)),
            full((n, d)),
            full((1, d)),
            per_head(LANES, d),
            per_head(n),
        ],
        out_specs=[full((n, d)), full((n, d)), per_head(n), full((8, d))],
        out_shape=[
            shape((n, d), F32),
            shape((n, d), BF16),
            shape((heads, n, LANES), BF16),
            shape((8, d), F32),
        ],
        scratch_shapes=[pltpu.VMEM((n, LANES), F32)],
        compiler_params=params(),
        cost_estimate=pl.CostEstimate(
            flops=2 * n * d * heads * LANES, bytes_accessed=20 * 2**20, transcendentals=0
        ),
        name="turn",
    )(place, cot, own_g, peer_g, hidden, gain, out_w, merged)


def pair_back(keys, q, do):
    weights = jnp.exp2(dot_rt(keys, q) * EXP_SCALE)
    inner = (weights * dot_rt(keys, do)).astype(BF16)
    grad_keys = dot(weights.astype(BF16), do) + dot(inner, q)
    return grad_keys, dot(keys.T, inner)


def peers_back_kernel(q, do, kv_all, dq, to_core, kept, acc):
    half = q.shape[1]
    n = 2 * half
    for level in (1, 2, 3, 4):
        count = n >> level
        start = (level - 1) * half
        for k in range(0, half, 256):
            grad, grad_q = pair_back(
                kv_all[0, pl.ds(start + k, 256), :], q[0, pl.ds(0, count), :], do[0, pl.ds(0, count), :]
            )
            if level == 1:
                to_core[0, pl.ds(k, 256), :] = grad.astype(BF16)
            elif level == 2:
                if k == 0:
                    kept[0, pl.ds(0, 256), :] = grad
                else:
                    to_core[0, pl.ds(half, 256), :] = grad.astype(BF16)
            else:
                unit = 256 >> 1
                off = 0 if level == 3 else unit
                one, two = grad[:unit], grad[unit:]
                if k == 0:
                    kept[0, pl.ds(256 + off, unit), :] = one
                    kept[0, pl.ds(512 + off, unit), :] = two
                else:
                    to_core[0, pl.ds(half + 256 + off, unit), :] = one.astype(BF16)
                    to_core[0, pl.ds(half + 512 + off, unit), :] = two.astype(BF16)
            if count >= LANES:
                if level == 1 and k == 0:
                    acc[...] = grad_q
                else:
                    acc[:, :count] += grad_q
            else:
                acc[:, :LANES] += jnp.concatenate(
                    [grad_q, jnp.zeros((LANES, LANES - count), F32)], axis=1
                )
    dq[0] = acc[...].T


def peers_back(q, do, kv_all):
    heads, n, _ = q.shape
    assert n == SEG
    return pl.pallas_call(
        peers_back_kernel,
        grid=(heads,),
        in_specs=[per_head(n // 2), per_head(n // 2), per_head(2 * n)],
        out_specs=[per_head(n // 2), per_head(n + n // 4), per_head(3 * n // 4)],
        out_shape=[
            shape((heads, n // 2, LANES), F32),
            shape((heads, n + n // 4, LANES), BF16),
            shape((heads, 3 * n // 4, LANES), F32),
        ],
        scratch_shapes=[pltpu.VMEM((LANES, n // 2), F32)],
        compiler_params=params(),
        cost_estimate=pl.CostEstimate(
            flops=heads * n * n * 1280, bytes_accessed=24 * 2**20, transcendentals=heads * n * n // 2
        ),
        name="peers_back",
    )(q, do, kv_all)


def own_back_kernel(q, do, kv, dq, dkv, acc, *, block):
    n = q.shape[1]
    for i in range(n // block):
        at = pl.ds(i * block, block)
        grad, grad_q = pair_back(kv[0, at, :], q[0], do[0])
        dkv[0, at, :] = grad
        if i == 0:
            acc[...] = grad_q
        else:
            acc[...] += grad_q
    dq[0] = acc[...].T


def own_back(q, do, kv):
    heads, n, _ = q.shape
    return pl.pallas_call(
        functools.partial(own_back_kernel, block=256),
        grid=(heads,),
        in_specs=[per_head(n)] * 3,
        out_specs=[per_head(n)] * 2,
        out_shape=[shape((heads, n, LANES), F32)] * 2,
        scratch_shapes=[pltpu.VMEM((LANES, n), F32)],
        compiler_params=params(),
        cost_estimate=pl.CostEstimate(
            flops=heads * n * n * 2560, bytes_accessed=16 * 2**20, transcendentals=heads * n * n
        ),
        name="own_back",
    )(q, do, kv)


def finish_kernel(
    place, dq_own, dq_peer, dkv_own, r_core, r_x, r_z1, r_z2, r_z3, normed, rows, wide,
    grad_normed, grad_w, grad_b, sums, acc, q_nat, kv_nat, both,
):
    h = pl.program_id(0)
    n, d = rows.shape
    block = n // FOLD
    head = place[0] + h
    for p in range(FOLD):
        c = (head + ORDER[p]) % FOLD
        at = pl.ds(p * block, block)
        q_rows = dq_own[0, at, :]
        kv_rows = dkv_own[0, at, :]
        if CLASS[p] >= 1:
            q_rows = q_rows + dq_peer[0, at, :]
            kv_rows = kv_rows + r_core[0, at, :].astype(F32)
        if CLASS[p] >= 2:
            kv_rows = kv_rows + r_x[0, at, :].astype(F32)
        if CLASS[p] >= 3:
            kv_rows = kv_rows + r_z1[0, at, :].astype(F32)
        if CLASS[p] >= 4:
            kv_rows = kv_rows + (r_z2[0, at, :].astype(F32) + r_z3[0, at, :].astype(F32))
        q_nat[pl.ds(c, block, stride=FOLD), :] = q_rows
        kv_nat[pl.ds(c, block, stride=FOLD), :] = kv_rows
    lane = lax.broadcasted_iota(jnp.int32, (n, LANES), 1)
    q_rows = jnp.where(lane < HD, q_nat[...] * (1.0 / ROOT), 0.0)
    kv_rows = kv_nat[...]
    kv_rows = jnp.where(lane < HD, kv_rows * (1.0 / ROOT), jnp.where(lane < 2 * HD, kv_rows, 0.0))
    grad_b[0, 0:1, :] = jnp.sum(q_rows, 0, keepdims=True)
    grad_b[0, 1:2, :] = jnp.sum(kv_rows, 0, keepdims=True)
    both[:, :LANES] = q_rows.astype(BF16)
    both[:, LANES:] = kv_rows.astype(BF16)
    gradient = dot_lt(both[...], normed[...])
    grad_w[0, 0] = gradient[:HD]
    grad_w[1, 0] = gradient[LANES : LANES + HD]
    grad_w[2, 0] = gradient[LANES + HD : LANES + 2 * HD]
    part = dot_rt(both[...], wide[0])

    @pl.when(h == 0)
    def _():
        acc[...] = part

    @pl.when(h > 0)
    def _():
        acc[...] += part

    @pl.when(h == pl.num_programs(0) - 1)
    def _():
        total = acc[...]
        grad_normed[...] = total.astype(BF16)
        unit, _ = unit_rows(rows[...].astype(F32))
        sums[0:1, :] = jnp.sum(total * unit, 0, keepdims=True)
        sums[1:2, :] = jnp.sum(total, 0, keepdims=True)
        sums[2:8, :] = jnp.zeros((6, d), F32)


def finish(place, dq_own, dq_peer, dkv_own, received, normed, rows, wide):
    heads, n, _ = dq_own.shape
    d = rows.shape[1]
    return pl.pallas_call(
        finish_kernel,
        grid=(heads,),
        in_specs=[
            pl.BlockSpec(memory_space=pltpu.SMEM),
            per_head(n),
            per_head(n // 2),
            per_head(n),
            per_head(n // 2),
            per_head(n // 4),
            per_head(n // 8),
            per_head(n // 16),
            per_head(n // 16),
            full((n, d)),
            full((n, d)),
            per_head(d, 2 * LANES),
        ],
        out_specs=[
            full((n, d)),
            pl.BlockSpec((3, 1, HD, d), lambda h: (0, h, 0, 0)),
            pl.BlockSpec((1, 2, LANES), lambda h: (h, 0, 0)),
            full((8, d)),
        ],
        out_shape=[
            shape((n, d), BF16),
            shape((3, heads, HD, d), F32),
            shape((heads, 2, LANES), F32),
            shape((8, d), F32),
        ],
        scratch_shapes=[
            pltpu.VMEM((n, d), F32),
            pltpu.VMEM((n, LANES), F32),
            pltpu.VMEM((n, LANES), F32),
            pltpu.VMEM((n, 2 * LANES), BF16),
        ],
        compiler_params=params(),
        cost_estimate=pl.CostEstimate(
            flops=4 * n * d * heads * 256, bytes_accessed=30 * 2**20, transcendentals=0
        ),
        name="finish",
    )(place, dq_own, dq_peer, dkv_own, *received, normed, rows, wide)


def last_kernel(rows, own_g, peer_g, grad_hidden, gain, out):
    unit, inverse = unit_rows(rows[...].astype(F32))
    gradient = own_g[...].astype(F32) + peer_g[...].astype(F32)
    out[...] = grad_hidden[...] + norm_back(gradient, unit, inverse, gain[...])


def last(rows, own_g, peer_g, grad_hidden, gain):
    n, d = rows.shape
    part = pl.BlockSpec((256, d), lambda i: (i, 0))
    return pl.pallas_call(
        last_kernel,
        grid=(n // 256,),
        in_specs=[part] * 4 + [full((1, d))],
        out_specs=part,
        out_shape=shape((n, d), F32),
        compiler_params=params(),
        name="last",
    )(rows, own_g, peer_g, grad_hidden, gain)


def swap(x, axis, apart):
    count = lax.axis_size(axis)
    return lax.ppermute(x, axis, [(i, i ^ apart) for i in range(count)])


def local(
    rows,
    lengths,
    norm_gains,
    norm_shifts,
    qkv_weight,
    qv_bias,
    out_weight,
    out_bias,
    up_weight,
    up_bias,
    down_weight,
    down_bias,
    out_cot,
):
    n, d = rows.shape
    width = qkv_weight.shape[2]
    heads = width // HD
    seq_place = lax.axis_index("seq")
    head_place = lax.axis_index("head")
    slide_rows = min(FOLD * SEG, n * lax.axis_size("seq"))
    start = seq_place * n
    slide = start // slide_rows
    length = jnp.sum(jnp.where(jnp.arange(lengths.shape[0]) == slide, lengths, 0))
    limit = jnp.clip(length - start % slide_rows, 0, n)
    place = jnp.stack([head_place * heads, limit, head_place]).astype(jnp.int32)

    peer_out_weight = swap(out_weight, "head", 1)
    wide_out = jnp.pad(
        out_weight.reshape(heads, HD, d), ((0, 0), (HD, LANES - 2 * HD), (0, 0))
    )

    q, kv, s1, sx, sz1, sz, normed1, wide = project(
        place, rows, norm_gains[:1], norm_shifts[:1], qkv_weight, qv_bias
    )
    rz1 = swap(sz1, "seq", 4)
    rx = swap(sx, "seq", 2)
    rz2 = swap(sz, "seq", 8)
    rz3 = swap(sz, "seq", 12)
    cs1 = swap(s1, "seq", 1)
    zc = jnp.concatenate([rz1, rz2, rz3], 1)
    rx2 = swap(zc, "seq", 2)
    crx = swap(rx, "seq", 1)
    czc = swap(zc, "seq", 1)
    crx2 = swap(rx2, "seq", 1)

    own = own_attention(q, kv)
    merged, kv_all, qb, merged_low = peers_attention(
        place, q, own, (cs1, rx, crx, zc, rx2, czc, crx2)
    )
    peer_low = swap(merged_low, "head", 1)

    hidden, normed2, act, grad_pre, grad_normed2, up_bias_grad = feed(
        place,
        rows,
        out_cot,
        merged_low,
        peer_low,
        out_weight,
        peer_out_weight,
        out_bias[None],
        norm_gains[1:],
        norm_shifts[1:],
        up_weight,
        up_bias[None],
        down_weight,
    )
    peer_normed2 = swap(grad_normed2, "head", 1)
    mlp = dot(act, down_weight).astype(BF16)
    down_weight_grad = dot_lt(act, out_cot)
    up_weight_grad = dot_lt(normed2, grad_pre)
    peer_mlp = swap(mlp, "head", 1)
    out_rows = (
        hidden + ((mlp.astype(F32) + peer_mlp.astype(F32)) + down_bias)
    ).astype(BF16)

    grad_hidden, grad_low, do, sums2 = turn(
        place, out_cot, grad_normed2, peer_normed2, hidden, norm_gains[1:], wide_out, merged
    )
    out_weight_grad = dot_lt(merged_low, grad_low)

    dq_peer, to_core, kept = peers_back(qb, do, kv_all)
    r_core = swap(to_core, "seq", 1)
    half = n // 2
    quarter = n // 4

    def both(at):
        return (
            kept[:, at : at + quarter] + r_core[:, half + at : half + at + quarter].astype(F32)
        )

    r_x2 = swap(both(2 * quarter).astype(BF16), "seq", 2)
    r_x = swap(both(0).astype(BF16), "seq", 2)
    z_sum = (both(quarter) + r_x2.astype(F32)).astype(BF16)
    eighth = n // 8
    r_z1 = swap(z_sum[:, :eighth], "seq", 4)
    r_z2 = swap(z_sum[:, eighth : eighth + n // 16], "seq", 8)
    r_z3 = swap(z_sum[:, eighth + n // 16 :], "seq", 12)

    dq_own, dkv_own = own_back(qb, do, kv)
    grad_normed1, grad_w, grad_b, sums1 = finish(
        place, dq_own, dq_peer, dkv_own, (r_core, r_x, r_z1, r_z2, r_z3), normed1, rows, wide
    )
    peer_normed1 = swap(grad_normed1, "head", 1)
    rows_grad = last(rows, grad_normed1, peer_normed1, grad_hidden, norm_gains[:1])

    up_weight_grad, down_weight_grad, out_weight_grad = (
        g.astype(F32)
        for g in lax.psum(
            tuple(g.astype(BF16) for g in (up_weight_grad, down_weight_grad, out_weight_grad)),
            "seq",
        )
    )
    grad_w = lax.psum(grad_w.astype(BF16), "seq").astype(F32)
    qkv_grad = jnp.swapaxes(grad_w.reshape(3, width, d), 1, 2)
    qv_bias_grad = jnp.stack(
        [grad_b[:, 0, :HD].reshape(width), grad_b[:, 1, HD : 2 * HD].reshape(width)]
    )
    up_bias_grad, qv_bias_grad, sums2 = lax.psum((up_bias_grad, qv_bias_grad, sums2), "seq")
    sums1 = lax.psum(sums1, ("seq", "head"))
    return (
        out_rows,
        rows_grad,
        jnp.stack([sums1[0], sums2[0]]),
        jnp.stack([sums1[1], sums2[1]]),
        qkv_grad,
        qv_bias_grad,
        out_weight_grad,
        sums2[2],
        up_weight_grad,
        up_bias_grad[0],
        down_weight_grad,
        sums2[3],
    )


def solution(mesh):
    placed = (
        P("seq", None),
        P(),
        P(),
        P(),
        P(None, None, "head"),
        P(None, "head"),
        P("head", None),
        P(),
        P(None, "head"),
        P("head"),
        P("head", None),
        P(),
        P("seq", None),
    )
    return jax.shard_map(
        local,
        mesh=mesh,
        in_specs=placed,
        out_specs=(
            P("seq", None),
            P("seq", None),
            P(),
            P(),
            P(None, None, "head"),
            P(None, "head"),
            P("head", None),
            P(),
            P(None, "head"),
            P("head"),
            P("head", None),
            P(),
        ),
        check_vma=False,
    )
```

time: 1470 us -> 489 us (0.33); the launches traced: 1450 us -> 488 us
  local copies, waits for them, and re-layouts: 457 us -> 15.2 us
  matrix products: 321 us -> 16 us
  other arithmetic: 242 us -> 20.2 us
  waiting for transfers between devices: 302 us -> 130 us
  Pallas kernels: 0 us -> 150 us
  blocking collectives: 64.8 us -> 121 us
  starting transfers between devices: 42.7 us -> 21.7 us
    dot_general x172 -> x4, matrix products: 321 us -> 16 us  [the longest x3 9.6 us: dot_lt(): lax.dot_general(left, right, (((0,), (0,)), ((), ())), preferred_element_...]
    psum x4 -> x1, waiting for transfers between devices: 285 us -> 0.01 us  [local(): grad_w = lax.psum(grad_w.astype(BF16), 'seq').astype(F32)]
    mul x59 -> x0, local copies, waits for them, and re-layouts: 155 us -> none  [the longest x54 153 us: place_rows(): spread = moved_rows[:, None] * select_mask]
    pallas_call x0 -> x9, Pallas kernels: none -> 150 us  [the longest x1 24.4 us: own_back(): pl.pallas_call(functools.partial(own_back_kernel, block=256), grid=(heads...]
    ppermute x50 -> x20, waiting for transfers between devices: 17.4 us -> 130 us  [swap(): return lax.ppermute(x, axis, [(i, i ^ apart) for i in range(count)])]
    reduce_sum x50 -> x0, other arithmetic: 95.4 us -> none  [the longest x16 46.8 us: select_rows(): chosen = jnp.sum(folded * select_mask, axis=1)]
    psum x1 -> x2, blocking collectives: 64.8 us -> 121 us  [the longest x1 60.9 us: local(): lax.psum((up_bias_grad, qv_bias_grad, sums2), 'seq')]
    select_n x39 -> x0, other arithmetic: 47.8 us -> none  [the longest x33 45.5 us: join_halves(): jnp.where(is_upper, jnp.concatenate([peer_piece, own_piece], 1), jnp.conc...]
  transfers between devices with their start and end apart: 54 -> 21, of which waited for: 15 -> 9; matrix products, arithmetic and copies ran while one was open for 51% -> 5% of each run, Pallas kernels for 0% -> 9%
where the time goes in v1:
time: 489 us; the launch traced here: 488 us
  Pallas kernels  150 us (31%)
  waiting for transfers between devices  130 us (27%)
  blocking collectives  121 us (25%)
  starting transfers between devices  21.7 us (4%)
  other arithmetic  20.2 us (4%)
  matrix products  16 us (3%)
  local copies, waits for them, and re-layouts  15.2 us (3%)
  between operations  14.9 us (3%)
    ppermute x20, waiting for transfers between devices, swap(): return lax.ppermute(x, axis, [(i, i ^ apart) for i in range(count)])  130 us
    psum x1, blocking collectives, local(): lax.psum((up_bias_grad, qv_bias_grad, sums2), 'seq')  60.9 us
    psum x1, blocking collectives, local(): sums1 = lax.psum(sums1, ('seq', 'head'))  59.9 us
    pallas_call x1, Pallas kernels, own_back(): pl.pallas_call(functools.partial(own_back_kernel, block=256), grid=(heads...  24.4 us
    ppermute x20, starting transfers between devices, swap(): return lax.ppermute(x, axis, [(i, i ^ apart) for i in range(count)])  21.7 us
    pallas_call x1, Pallas kernels, peers_back(): pl.pallas_call(peers_back_kernel, grid=(heads,), in_specs=[per_head(n //...  20.7 us
    pallas_call x1, Pallas kernels, finish(): pl.pallas_call(finish_kernel, grid=(heads,), in_specs=[pl.BlockSpec(memor...  19.1 us
    pallas_call x1, Pallas kernels, peers_attention(): pl.pallas_call(peers_kernel, grid=(heads,), in_specs=[pl.BlockSpec(memory...  18.2 us
  transfers between devices with their start and end apart: 21, of which 9 were waited for; matrix products, arithmetic and copies ran while one was open for 5% of the time, Pallas kernels for 9%

profile of v1, /device:TPU:0, one launch (start us, length us, event | category | flops | bytes accessed | tf_op | source)
XLA Modules:
  0.0 488.1 jit_solution(8755104670616710630)
XLA Ops:
  11.6 15.4 %project.1 = (bf16[8,1024,128]{2,1,0:T(8,128)(2,1)}, bf16[8,1024,128]{2,1,0:T(8,128)(2,1)}, bf16[8,512,128]{2,1,0:T(8,128)(2,1)S(1)}, bf16[8,256,128]{2,1,0:T(8,...) custom-call(s32[3]{0:T(128)S(1)} %pad_add_fusion.place, ...), custom_call_target="tpu_custom_call" | custom-call | flops 3221225472 | bytes 14680064 | tf_op jit(solution)/shard_map/project/pallas_call | solution.py:194
  28.1 3.0 collective-permute-start.3
  31.1 2.6 collective-permute-start.4
  33.7 1.7 collective-permute-start.1
  35.4 4.8 collective-permute-done.3
  40.7 4.6 collective-permute-done.5
  47.5 10.7 %collective-permute-done.6.rx2 = bf16[8,256,128]{2,1,0:T(8,128)(2,1)S(1)} collective-permute-done((bf16[8,256,128]{2,1,0:T(8,128)(2,1)S(1)}, bf16[8,256,128]{2,1,0:T(8,128)(2,1)S(1)}, u32[]{:S(2)}, u32[]{:S(2)}) %collective-permute-start.6) | collective-permute-done | bytes 524320 | tf_op jit(solution)/shard_map/ppermute | solution.py:720
  61.4 12.5 %own_attention.1.own = f32[8,1024,128]{2,1,0:T(8,128)} custom-call(bf16[8,1024,128]{2,1,0:T(8,128)(2,1)S(1)} %copy-done.12, bf16[8,1024,128]{2,1,0:T(8,128)(2,1)S(1)} %copy-done.14), custom_call_target="tpu_custom_call" | custom-call | flops 8589934592 | bytes 8388608 | tf_op jit(solution)/shard_map/own_attention/pallas_call | solution.py:243
  74.0 18.2 %peers_attention.1 = (f32[8,1024,128]{2,1,0:T(8,128)}, bf16[8,2048,128]{2,1,0:T(8,128)(2,1)}, bf16[8,1024,128]{2,1,0:T(8,128)(2,1)}, bf16[1024,384]{1,0:T(8,128)(2,1)S(1)}) custom-call(s32[3]{0:T(128)S(1)} %pad_add_fusion.place, bf16[8,1024,128]{2,1,0:T(8,128)(2,1)} %get-tuple-element.43.q, f32[8,1024,128]{2,1,0:T(8,128)} %own_attention.1.own, ...), custom_call_target="tpu_custom_call" | custom-call | flops 4294967296 | bytes 25165824 | tf_op jit(solution)/shard_map/peers_attention/pallas_call | solution.py:326
  94.2 30.5 %collective-permute-done.10.peer_w = bf16[384,768]{1,0:T(8,128)(2,1)S(1)} collective-permute-done((bf16[384,768]{1,0:T(8,128)(2,1)S(1)}, bf16[384,768]{1,0:T(8,128)(2,1)S(1)}, u32[]{:S(2)}, u32[]{:S(2)}) %collective-permute-start.10) | collective-permute-done | bytes 589856 | tf_op jit(solution)/shard_map/ppermute | solution.py:720
  124.8 17.4 %feed_forward.1 = (f32[1024,768]{1,0:T(8,128)}, bf16[1024,768]{1,0:T(8,128)(2,1)S(1)}, bf16[1024,1536]{1,0:T(8,128)(2,1)}, bf16[1024,1536]{1,0:T(8,128)(2,1)}, b...) custom-call(s32[3]{0:T(128)S(1)} %pad_add_fusion.place, bf16[1024,768]{1,0:T(8,128)(2,1)} %rows.7, ...), custom_call_target="tpu_custom_call" | custom-call | flops 8455716864 | bytes 25165824 | tf_op jit(solution)/shard_map/feed_forward/pallas_call | solution.py:398
  144.9 33.3 %collective-permute-done.12.peer_g = bf16[1024,768]{1,0:T(8,128)(2,1)S(1)} collective-permute-done((bf16[1024,768]{1,0:T(8,128)(2,1)S(1)}, bf16[1024,768]{1,0:T(8,128)(2,1)S(1)}, u32[]{:S(2)}, u32[]{:S(2)}) %collective-permute-start.12) | collective-permute-done | bytes 1572896 | tf_op jit(solution)/shard_map/ppermute | solution.py:720
  179.4 16.3 %turn.1 = (f32[1024,768]{1,0:T(8,128)}, bf16[1024,768]{1,0:T(8,128)(2,1)S(1)}, bf16[8,1024,128]{2,1,0:T(8,128)(2,1)}, f32[8,768]{1,0:T(8,128)S(1)}) custom-call(s32[3]{0:T(128)S(1)} %pad_add_fusion.place, bf16[1024,768]{1,0:T(8,128)(2,1)S(1)} %copy-done, bf16[1024,768]{1,0:T(8,128)(2,1)S(1)} %get-tuple-element.53.own_g, bf16[1024,768]{1,0:T(8,128)(2,1)} %copy-done.18, ...), custom_call_target="tpu_custom_call" | custom-call | flops 1610612736 | bytes 20971520 | tf_op jit(solution)/shard_map/turn/pallas_call | solution.py:469
  195.7 20.7 %peers_back.1 = (f32[8,512,128]{2,1,0:T(8,128)S(1)}, bf16[8,1280,128]{2,1,0:T(8,128)(2,1)}, f32[8,768,128]{2,1,0:T(8,128)}) custom-call(bf16[8,1024,128]{2,1,0:T(8,128)(2,1)S(1)} %copy-done.13, bf16[8,1024,128]{2,1,0:T(8,128)(2,1)} %get-tuple-element.55.do, bf16[8,2048,128]{2,1,0:T(8,128)(2,1)} %get-tuple-element.57.kv_all), custom_call_target="tpu_custom_call" | custom-call | flops 10737418240 | bytes 25165824 | tf_op jit(solution)/shard_map/peers_back/pallas_call | solution.py:547
  216.5 4.0 convolution_convert_fusion
  220.4 4.0 convolution_convert_fusion.1
  226.1 24.4 %own_back.1 = (f32[8,1024,128]{2,1,0:T(8,128)}, f32[8,1024,128]{2,1,0:T(8,128)}) custom-call(bf16[8,1024,128]{2,1,0:T(8,128)(2,1)S(1)} %copy-done.13, bf16[8,1024,128]{2,1,0:T(8,128)(2,1)S(1)} %copy-done.4, bf16[8,1024,128]{2,1,0:T(8,128)(2,1)} %get-tuple-element.44.kv), custom_call_target="tpu_custom_call" | custom-call | flops 21474836480 | bytes 16777216 | tf_op jit(solution)/shard_map/own_back/pallas_call | solution.py:581
  252.3 3.6 collective-permute-start.17
  257.8 4.0 collective-permute-done.17.r_z2
  261.8 5.6 %collective-permute-done.18.r_z3 = bf16[8,64,128]{2,1,0:T(8,128)(2,1)S(1)} collective-permute-done((bf16[8,64,128]{2,1,0:T(8,128)(2,1)S(1)}, bf16[8,64,128]{2,1,0:T(8,128)(2,1)S(1)}, u32[]{:S(2)}, u32[]{:S(2)}) %collective-permute-start.18) | collective-permute-done | bytes 131104 | tf_op jit(solution)/shard_map/ppermute | solution.py:720
  267.4 19.1 %finish.1 = (bf16[1024,768]{1,0:T(8,128)(2,1)S(1)}, f32[3,8,48,768]{3,2,1,0:T(8,128)}, f32[8,2,128]{2,1,0:T(2,128)S(1)}, f32[8,768]{1,0:T(8,128)S(1)}) custom-call(s32[3]{0:T(128)S(1)} %pad_add_fusion.place, f32[8,1024,128]{2,1,0:T(8,128)} %get-tuple-element.56.dq_own, f32[8,512,128]{2,1,0:T(8,128)} %copy-done.9, f32[8,1024,128]{2,1,0:T(8,128)} %get-tuple-element.59.dkv_own, ...), custom_call_target="tpu_custom_call" | custom-call | flops 6442450944 | bytes 31457280 | tf_op jit(solution)/shard_map/finish/pallas_call | solution.py:655
  286.6 3.4 convert_element_type.68
  289.9 3.8 copy.28
  293.8 6.4 %convolution_convert_fusion.2 = bf16[1024,768]{1,0:T(8,128)(2,1)} fusion(bf16[1024,1536]{1,0:T(8,128)(2,1)} %get-tuple-element.51, bf16[1536,768]{1,0:T(8,128)(2,1)} %down_w.1), kind=kOutput, calls=%fused_computation.3 | convolution fusion | flops 2416705536 | bytes 7077888 | tf_op jit(solution)/shard_map/dot_general | solution.py:42
  302.2 35.6 %collective-permute-done.11 = bf16[1024,768]{1,0:T(8,128)(2,1)} collective-permute-done((bf16[1024,768]{1,0:T(8,128)(2,1)}, bf16[1024,768]{1,0:T(8,128)(2,1)}, u32[]{:S(2)}, u32[]{:S(2)}) %collective-permute-start.11) | collective-permute-done | bytes 1572896 | tf_op jit(solution)/shard_map/ppermute | solution.py:720
  337.8 4.7 add_convert_fusion
  342.8 59.9 %psum.56 = f32[8,768]{1,0:T(8,128)S(1)} all-reduce(f32[8,768]{1,0:T(8,128)S(1)} %get-tuple-element.66), channel_id=1, replica_groups=mesh['seq'=16,'head'=2] {'seq','head'}, use_global_device_ids=true, to_apply=%region_0.1 | all-reduce | flops 6144 | bytes 49152 | tf_op jit(solution)/shard_map/psum | solution.py:842
  402.7 60.9 %all-reduce.1 = (f32[8,768]{1,0:T(8,128)S(1)}, f32[2,384]{1,0:T(2,128)}, f32[1536]{0:T(1024)}) all-reduce(f32[8,768]{1,0:T(8,128)S(1)} %get-tuple-element.67, f32[2,384]{1,0:T(2,128)S(1)} %pad_maximum_fusion.2, f32[1536]{0:T(1024)S(1)} %reduce.3), channel_id=1, replica_groups=mesh['seq'=16,'head'=2] {'seq'}, use_global_device_ids=true, to_apply=%region_1.2 | all-reduce | flops 8448 | bytes 67584 | tf_op jit(solution)/shard_map/psum | solution.py:841
  465.4 5.5 %last.1 = f32[1024,768]{1,0:T(8,128)} custom-call(bf16[1024,768]{1,0:T(8,128)(2,1)S(1)} %copy-done.2, bf16[1024,768]{1,0:T(8,128)(2,1)S(1)} %get-tuple-element.64.own_g, bf16[1024,768]{1,0:T(8,128)(2,1)} %collective-permute-done.19.peer_g, f32[1024,768]{1,0:T(8,128)} %get-tuple-element.65.grad_hidden, f32[1,768]{1,0:T(1,128)S(1)} %get-tuple-element.97.gain), custom_call_target="tpu_custom_call" | custom-call | tf_op jit(solution)/shard_map/last/pallas_call | solution.py:707
  470.9 4.6 convert_element_type.72
  475.6 2.5 convert_element_type.74
  478.1 2.0 transpose.10
  (106 shorter events, 27.2 us)
Async XLA Ops:
  7.2 463.7 %all-reduce.5.cloned.1.call-start = ((), (), s32[]{:S(2)}) async-start(), calls=%async_computation | async-start | bytes 14155776 | tf_op jit(solution)/shard_map/psum | solution.py:836
  28.1 12.1 %collective-permute-start.3 = (bf16[8,128,128]{2,1,0:T(8,128)(2,1)S(1)}, bf16[8,128,128]{2,1,0:T(8,128)(2,1)S(1)}, u32[]{:S(2)}, u32[]{:S(2)}) collective-permute-start(bf16[8,128,128]{2,1,0:T(8,128)(2,1)S(1)} %get-tuple-element.47), channel_id=1, source_target_pairs={{0,8},{2,10},{4,12},{6,14},{8,0},{10,2},{12,4},{14,6},{16,24},{18,... | collective-permute-start | bytes 786440 | tf_op jit(solution)/shard_map/ppermute | solution.py:720
  31.1 9.6 %collective-permute-start.4 = (bf16[8,64,128]{2,1,0:T(8,128)(2,1)S(1)}, bf16[8,64,128]{2,1,0:T(8,128)(2,1)S(1)}, u32[]{:S(2)}, u32[]{:S(2)}) collective-permute-start(bf16[8,64,128]{2,1,0:T(8,128)(2,1)S(1)} %get-tuple-element.48), channel_id=1, source_target_pairs={{0,16},{2,18},{4,20},{6,22},{8,24},{10,26},{12,28},{14,30},{16,0},... | collective-permute-start | bytes 393224 | tf_op jit(solution)/shard_map/ppermute | solution.py:720
  33.7 11.6 %collective-permute-start.5 = (bf16[8,64,128]{2,1,0:T(8,128)(2,1)S(1)}, bf16[8,64,128]{2,1,0:T(8,128)(2,1)S(1)}, u32[]{:S(2)}, u32[]{:S(2)}) collective-permute-start(bf16[8,64,128]{2,1,0:T(8,128)(2,1)S(1)} %get-tuple-element.48), channel_id=1, source_target_pairs={{0,24},{2,26},{4,28},{6,30},{8,16},{10,18},{12,20},{14,22},{16,8},... | collective-permute-start | bytes 393224 | tf_op jit(solution)/shard_map/ppermute | solution.py:720
  33.7 13.7 %collective-permute-start.1 = (bf16[8,256,128]{2,1,0:T(8,128)(2,1)S(1)}, bf16[8,256,128]{2,1,0:T(8,128)(2,1)S(1)}, u32[]{:S(2)}, u32[]{:S(2)}) collective-permute-start(bf16[8,256,128]{2,1,0:T(8,128)(2,1)S(1)} %get-tuple-element.46), channel_id=1, source_target_pairs={{0,4},{2,6},{4,0},{6,2},{8,12},{10,14},{12,8},{14,10},{16,20},{18,... | collective-permute-start | bytes 1572872 | tf_op jit(solution)/shard_map/ppermute | solution.py:720
  45.4 12.8 %collective-permute-start.6 = (bf16[8,256,128]{2,1,0:T(8,128)(2,1)S(1)}, bf16[8,256,128]{2,1,0:T(8,128)(2,1)S(1)}, u32[]{:S(2)}, u32[]{:S(2)}) collective-permute-start(bf16[8,256,128]{2,1,0:T(8,128)(2,1)S(1)} %constant_dynamic-update-slice_fusion.zc), channel_id=1, source_target_pairs={{0,4},{2,6},{4,0},{6,2},{8,12},{10,14},{12,8},{14,10},{16,20},{18,... | collective-permute-start | bytes 1572872 | tf_op jit(solution)/shard_map/ppermute | solution.py:720
  46.9 27.0 %collective-permute-start = (bf16[8,512,128]{2,1,0:T(8,128)(2,1)S(1)}, bf16[8,512,128]{2,1,0:T(8,128)(2,1)S(1)}, u32[]{:S(2)}, u32[]{:S(2)}) collective-permute-start(bf16[8,512,128]{2,1,0:T(8,128)(2,1)S(1)} %get-tuple-element.45), channel_id=1, source_target_pairs={{0,2},{2,0},{4,6},{6,4},{8,10},{10,8},{12,14},{14,12},{16,18},{18,... | collective-permute-start | bytes 3145736 | tf_op jit(solution)/shard_map/ppermute | solution.py:720
  46.9 27.0 %collective-permute-start.7 = (bf16[8,256,128]{2,1,0:T(8,128)(2,1)S(1)}, bf16[8,256,128]{2,1,0:T(8,128)(2,1)S(1)}, u32[]{:S(2)}, u32[]{:S(2)}) collective-permute-start(bf16[8,256,128]{2,1,0:T(8,128)(2,1)S(1)} %constant_dynamic-update-slice_fusion.zc), channel_id=1, source_target_pairs={{0,2},{2,0},{4,6},{6,4},{8,10},{10,8},{12,14},{14,12},{16,18},{18,... | collective-permute-start | bytes 1572872 | tf_op jit(solution)/shard_map/ppermute | solution.py:720
  47.5 26.5 %collective-permute-start.2 = (bf16[8,256,128]{2,1,0:T(8,128)(2,1)S(1)}, bf16[8,256,128]{2,1,0:T(8,128)(2,1)S(1)}, u32[]{:S(2)}, u32[]{:S(2)}) collective-permute-start(bf16[8,256,128]{2,1,0:T(8,128)(2,1)S(1)} %collective-permute-done.1.rx), channel_id=1, source_target_pairs={{0,2},{2,0},{4,6},{6,4},{8,10},{10,8},{12,14},{14,12},{16,18},{18,... | collective-permute-start | bytes 1572872 | tf_op jit(solution)/shard_map/ppermute | solution.py:720
  58.2 15.8 %collective-permute-start.8 = (bf16[8,256,128]{2,1,0:T(8,128)(2,1)S(1)}, bf16[8,256,128]{2,1,0:T(8,128)(2,1)S(1)}, u32[]{:S(2)}, u32[]{:S(2)}) collective-permute-start(bf16[8,256,128]{2,1,0:T(8,128)(2,1)S(1)} %collective-permute-done.6.rx2), channel_id=1, source_target_pairs={{0,2},{2,0},{4,6},{6,4},{8,10},{10,8},{12,14},{14,12},{16,18},{18,... | collective-permute-start | bytes 1572872 | tf_op jit(solution)/shard_map/ppermute | solution.py:720
  61.4 12.6 %copy-start.7 = (f32[32,128]{1,0:T(8,128)S(1)}, f32[32,128]{1,0:T(8,128)}, u32[]{:S(2)}) copy-start(f32[32,128]{1,0:T(8,128)} %constant.52.clone.table) | copy-start | bytes 49156
  73.9 19.7 %copy-start.3 = (bf16[384,768]{1,0:T(8,128)(2,1)S(1)}, bf16[384,768]{1,0:T(8,128)(2,1)}, u32[]{:S(2)}) copy-start(bf16[384,768]{1,0:T(8,128)(2,1)} %own_w.1) | copy-start | bytes 1769476
  73.9 20.3 %copy-start.21 = (f32[1536]{0:T(1024)S(1)}, f32[1536]{0:T(1024)}, u32[]{:S(2)}) copy-start(f32[1536]{0:T(1024)} %param.25) | copy-start | bytes 18436
  73.9 20.3 %copy-start.23 = (f32[768]{0:T(1024)S(1)}, f32[768]{0:T(1024)}, u32[]{:S(2)}) copy-start(f32[768]{0:T(1024)} %param.23) | copy-start | bytes 9220
  92.2 32.6 %collective-permute-start.9 = (bf16[1024,384]{1,0:T(8,128)(2,1)S(1)}, bf16[1024,384]{1,0:T(8,128)(2,1)S(1)}, u32[]{:S(2)}, u32[]{:S(2)}) collective-permute-start(bf16[1024,384]{1,0:T(8,128)(2,1)S(1)} %get-tuple-element.49.own_c), channel_id=1, source_target_pairs={{0,1},{1,0},{2,3},{3,2},{4,5},{5,4},{6,7},{7,6},{8,9},{9,8},{10,11... | collective-permute-start | bytes 2359304 | tf_op jit(solution)/shard_map/ppermute | solution.py:720
  93.6 31.1 %collective-permute-start.10 = (bf16[384,768]{1,0:T(8,128)(2,1)S(1)}, bf16[384,768]{1,0:T(8,128)(2,1)S(1)}, u32[]{:S(2)}, u32[]{:S(2)}) collective-permute-start(bf16[384,768]{1,0:T(8,128)(2,1)S(1)} %copy-done.3), channel_id=1, source_target_pairs={{0,1},{1,0},{2,3},{3,2},{4,5},{5,4},{6,7},{7,6},{8,9},{9,8},{10,11... | collective-permute-start | bytes 1769480 | tf_op jit(solution)/shard_map/ppermute | solution.py:720
  142.2 37.2 %copy-start = (bf16[1024,768]{1,0:T(8,128)(2,1)S(1)}, bf16[1024,768]{1,0:T(8,128)(2,1)}, u32[]{:S(2)}) copy-start(bf16[1024,768]{1,0:T(8,128)(2,1)} %cot.3) | copy-start | bytes 4718596
  142.2 36.0 %collective-permute-start.12 = (bf16[1024,768]{1,0:T(8,128)(2,1)S(1)}, bf16[1024,768]{1,0:T(8,128)(2,1)S(1)}, u32[]{:S(2)}, u32[]{:S(2)}) collective-permute-start(bf16[1024,768]{1,0:T(8,128)(2,1)S(1)} %get-tuple-element.53.own_g), channel_id=1, source_target_pairs={{0,1},{1,0},{2,3},{3,2},{4,5},{5,4},{6,7},{7,6},{8,9},{9,8},{10,11... | collective-permute-start | bytes 4718600 | tf_op jit(solution)/shard_map/ppermute | solution.py:720
  179.4 16.3 %copy-start.13 = (bf16[8,1024,128]{2,1,0:T(8,128)(2,1)S(1)}, bf16[8,1024,128]{2,1,0:T(8,128)(2,1)}, u32[]{:S(2)}) copy-start(bf16[8,1024,128]{2,1,0:T(8,128)(2,1)} %get-tuple-element.52.q) | copy-start | bytes 6291460
  195.7 20.8 %copy-start.25 = (bf16[1024,1536]{1,0:T(8,128)(2,1)S(1)}, bf16[1024,1536]{1,0:T(8,128)(2,1)}, u32[]{:S(2)}) copy-start(bf16[1024,1536]{1,0:T(8,128)(2,1)} %get-tuple-element.51) | copy-start | bytes 9437188
  216.4 8.0 %collective-permute-start.13 = (bf16[8,1280,128]{2,1,0:T(8,128)(2,1)}, bf16[8,1280,128]{2,1,0:T(8,128)(2,1)S(1)}, u32[]{:S(2)}, u32[]{:S(2)}) collective-permute-start(bf16[8,1280,128]{2,1,0:T(8,128)(2,1)} %get-tuple-element.60), channel_id=1, source_target_pairs={{0,2},{2,0},{4,6},{6,4},{8,10},{10,8},{12,14},{14,12},{16,18},{18,... | collective-permute-start | bytes 7864328 | tf_op jit(solution)/shard_map/ppermute | solution.py:720
  224.4 26.1 %copy-start.19 = (bf16[8,1280,128]{2,1,0:T(8,128)(2,1)}, bf16[8,1280,128]{2,1,0:T(8,128)(2,1)S(1)}, u32[]{:S(2)}) copy-start(bf16[8,1280,128]{2,1,0:T(8,128)(2,1)S(1)} %collective-permute-done.13.r_core) | copy-start | bytes 7864324
  224.6 25.9 %collective-permute-start.15 = (bf16[8,256,128]{2,1,0:T(8,128)(2,1)S(1)}, bf16[8,256,128]{2,1,0:T(8,128)(2,1)S(1)}, u32[]{:S(2)}, u32[]{:S(2)}) collective-permute-start(bf16[8,256,128]{2,1,0:T(8,128)(2,1)S(1)} %add_convert_fusion.2), channel_id=1, source_target_pairs={{0,4},{2,6},{4,0},{6,2},{8,12},{10,14},{12,8},{14,10},{16,20},{18,... | collective-permute-start | bytes 1572872 | tf_op jit(solution)/shard_map/ppermute | solution.py:720
  250.9 16.5 %copy-start.2 = (bf16[1024,768]{1,0:T(8,128)(2,1)S(1)}, bf16[1024,768]{1,0:T(8,128)(2,1)}, u32[]{:S(2)}) copy-start(bf16[1024,768]{1,0:T(8,128)(2,1)} %rows.7) | copy-start | bytes 4718596
  250.9 16.5 %copy-start.11 = (bf16[1024,768]{1,0:T(8,128)(2,1)S(1)}, bf16[1024,768]{1,0:T(8,128)(2,1)}, u32[]{:S(2)}) copy-start(bf16[1024,768]{1,0:T(8,128)(2,1)} %copy-done.10) | copy-start | bytes 4718596
  250.9 16.5 %collective-permute-start.14 = (bf16[8,256,128]{2,1,0:T(8,128)(2,1)S(1)}, bf16[8,256,128]{2,1,0:T(8,128)(2,1)S(1)}, u32[]{:S(2)}, u32[]{:S(2)}) collective-permute-start(bf16[8,256,128]{2,1,0:T(8,128)(2,1)S(1)} %get-tuple-element.86), channel_id=1, source_target_pairs={{0,4},{2,6},{4,0},{6,2},{8,12},{10,14},{12,8},{14,10},{16,20},{18,... | collective-permute-start | bytes 1572872 | tf_op jit(solution)/shard_map/ppermute | solution.py:720
  251.7 15.7 %collective-permute-start.16 = (bf16[8,128,128]{2,1,0:T(8,128)(2,1)S(1)}, bf16[8,128,128]{2,1,0:T(8,128)(2,1)S(1)}, u32[]{:S(2)}, u32[]{:S(2)}) collective-permute-start(bf16[8,128,128]{2,1,0:T(8,128)(2,1)S(1)} %slice.89), channel_id=1, source_target_pairs={{0,8},{2,10},{4,12},{6,14},{8,0},{10,2},{12,4},{14,6},{16,24},{18,... | collective-permute-start | bytes 786440 | tf_op jit(solution)/shard_map/ppermute | solution.py:720
  252.3 9.5 %collective-permute-start.17 = (bf16[8,64,128]{2,1,0:T(8,128)(2,1)S(1)}, bf16[8,64,128]{2,1,0:T(8,128)(2,1)S(1)}, u32[]{:S(2)}, u32[]{:S(2)}) collective-permute-start(bf16[8,64,128]{2,1,0:T(8,128)(2,1)S(1)} %get-tuple-element.88), channel_id=1, source_target_pairs={{0,16},{2,18},{4,20},{6,22},{8,24},{10,26},{12,28},{14,30},{16,0},... | collective-permute-start | bytes 393224 | tf_op jit(solution)/shard_map/ppermute | solution.py:720
  255.9 11.5 %collective-permute-start.18 = (bf16[8,64,128]{2,1,0:T(8,128)(2,1)S(1)}, bf16[8,64,128]{2,1,0:T(8,128)(2,1)S(1)}, u32[]{:S(2)}, u32[]{:S(2)}) collective-permute-start(bf16[8,64,128]{2,1,0:T(8,128)(2,1)S(1)} %get-tuple-element.87), channel_id=1, source_target_pairs={{0,24},{2,26},{4,28},{6,30},{8,16},{10,18},{12,20},{14,22},{16,8},... | collective-permute-start | bytes 393224 | tf_op jit(solution)/shard_map/ppermute | solution.py:720
  293.8 44.0 %copy-start.22 = (f32[768]{0:T(1024)S(1)}, f32[768]{0:T(1024)}, u32[]{:S(2)}) copy-start(f32[768]{0:T(1024)} %param.27) | copy-start | bytes 9220
  300.2 37.7 %collective-permute-start.11 = (bf16[1024,768]{1,0:T(8,128)(2,1)}, bf16[1024,768]{1,0:T(8,128)(2,1)}, u32[]{:S(2)}, u32[]{:S(2)}) collective-permute-start(bf16[1024,768]{1,0:T(8,128)(2,1)} %convolution_convert_fusion.2), channel_id=1, source_target_pairs={{0,1},{1,0},{2,3},{3,2},{4,5},{5,4},{6,7},{7,6},{8,9},{9,8},{10,11... | collective-permute-start | bytes 4718600 | tf_op jit(solution)/shard_map/ppermute | solution.py:720
  301.6 163.8 %collective-permute-start.19 = (bf16[1024,768]{1,0:T(8,128)(2,1)S(1)}, bf16[1024,768]{1,0:T(8,128)(2,1)}, u32[]{:S(2)}, u32[]{:S(2)}) collective-permute-start(bf16[1024,768]{1,0:T(8,128)(2,1)S(1)} %get-tuple-element.64.own_g), channel_id=1, source_target_pairs={{0,1},{1,0},{2,3},{3,2},{4,5},{5,4},{6,7},{7,6},{8,9},{9,8},{10,11... | collective-permute-start | bytes 4718600 | tf_op jit(solution)/shard_map/ppermute | solution.py:720
  (15 other events, 47.8 us)
Sparse Core Ops, SparseCore 0:
  293.9 151.1 all-reduce.4
